TPU v7x, 512 devices: a whole 4x4x16 slice. The times are simulated.
512 devices in a mesh: sec: 16 (over z), row: 32 (over x, y, core).
Axes of the slice: x: 4, y: 4, z: 16, core: 2. Of those that a mesh axis runs over, the one named last changes fastest.
Arguments:
- right_sides: bfloat16 [3072, 128, 256], P(('sec', 'row')), may hold values from -6 to 6
- inverses: bfloat16 [3072, 128, 128], P(('sec', 'row')), may hold values from -0.25 to 1.25, as said below
- coupling: bfloat16 [3072, 5, 128, 128], P(('sec', 'row')), may hold values from -0.1875 to 0.1875
- supernode_blocks: bfloat16 [7680, 128, 128], P(('sec', 'row')), may hold values from -0.109375 to 0.109375
- pattern: int32 [3072, 5], P(('sec', 'row')), may hold values from 0 to 191, as said below
Outputs:
- solution: bfloat16 [3072, 128, 256], P(('sec', 'row'))
Inputs may be any that keep to these rules, and one draw needn't show every extreme that they name: `pattern`: block row 192 s + 6 d + a lists 5 distinct positions, all within 6 d - 1 to 6 d + 6, one of them 6 d + a; the lists of section 0 are unused. `inverses`: each block is lower triangular with unit diagonal.
All inputs are finite; a program needn't handle non-finite values.
Results may differ from a plain program's by a relative error of at most 0.027.
Values may be sent and summed in bfloat16 or wider, within the bound.
No kernel may reach another device: no remote copies, remote signals or barrier semaphores. Data moves between devices by JAX's collectives and lax.ppermute only.
A program may use at most 64 MiB of HBM per device.

v0:
```python
import jax
import jax.numpy as jnp
from jax import lax
from jax.sharding import PartitionSpec as P

BD = 6


def shifted(block, axis, distance):
    devices = range(lax.axis_size(axis))
    route = [(i - distance, i) for i in devices if i - distance in devices]
    return lax.ppermute(block, axis, route)


def with_halo(x, sides, width):
    for axis, dim in sides:
        count, length = (lax.axis_size(axis), x.shape[dim])
        up = [(i, (i + 1) % count) for i in range(count - 1)]
        down = [(j, i) for i, j in up]
        last = lax.slice_in_dim(x, length - width, length, axis=dim)
        initial = lax.slice_in_dim(x, 0, width, axis=dim)
        before = lax.ppermute(last, axis, up)
        after = lax.ppermute(initial, axis, down)
        x = jnp.concatenate([before, x, after], axis=dim)
    return x


def local(right_sides, inverses, coupling, supernode_blocks, pattern):
    row_index = lax.axis_index("row")
    sections = lax.axis_size("sec")
    offsets = pattern - (row_index * BD - 1)

    def neighbours(latest):
        incoming = shifted(latest, "sec", 1)
        window = with_halo(incoming, (("row", 0),), 1)
        return window

    def supernode(window, rhs_portion):
        picked = jnp.take(window, offsets, axis=0)
        updates = lax.dot_general(
            coupling, picked, (((1, 3), (1, 2)), ((0,), (0,))), preferred_element_type=jnp.float32
        )
        remain = rhs_portion.astype(jnp.float32) - updates
        solved = []
        for a in range(BD):
            residue = remain[a]
            for b in range(a):
                residue = residue - jnp.dot(
                    supernode_blocks[a * (a - 1) // 2 + b],
                    solved[b],
                    preferred_element_type=jnp.float32,
                )
            value = jnp.dot(
                inverses[a], residue.astype(jnp.bfloat16), preferred_element_type=jnp.float32
            )
            solved.append(value.astype(jnp.bfloat16))
        return jnp.stack(solved, axis=0)

    def advance(step, current):
        window = neighbours(current)
        return supernode(window, right_sides)

    solution = lax.fori_loop(0, sections, advance, jnp.zeros_like(right_sides))
    return solution


def solution(mesh):
    return jax.shard_map(
        local,
        mesh=mesh,
        in_specs=(
            P(("sec", "row"), None, None),
            P(("sec", "row"), None, None),
            P(("sec", "row"), None, None, None),
            P(("sec", "row"), None, None),
            P(("sec", "row"), None),
        ),
        out_specs=P(("sec", "row"), None, None),
        check_vma=False,
    )
```

profile of v0, /device:TPU:390, one launch (start us, length us, event | category | flops | bytes accessed | tf_op | source)
XLA Modules:
  0.0 515.8 jit_solution(14713119460469532786)
XLA Ops:
  3.4 510.5 %while.10 = (s32[]{:T(128)}, bf16[6,128,256]{1,2,0:T(8,128)(2,1)}, bf16[6,128,256]{1,2,0:T(8,128)(2,1)}, s32[6,5]{1,0:T(8,128)S(1)}, bf16[6,5,128,128]{3,2,1,0:T...) while((s32[]{:T(128)}, bf16[6,128,256]{1,2,0:T(8,128)(2,1)}, ...), condition=%wide.region_1.0_spmd, body=%wide.region_0.1_spmd.sunk | while | flops 430572800 | bytes 19960968 | solution.py:63
  3.4 2.9 collective-permute-start
  6.4 11.1 %collective-permute-done = bf16[6,128,256]{1,2,0:T(8,128)(2,1)S(1)} collective-permute-done((bf16[6,128,256]{1,2,0:T(8,128)(2,1)}, bf16[6,128,256]{1,2,0:T(8,128)(2,1)S(1)}, u32[]{:S(2)}, u32[]{:S(2)}) %collective-permute-start) | collective-permute-done | bytes 393248 | tf_op jit(solution)/shard_map/while/body/eval_jaxpr/ppermute | solution.py:12
  17.6 3.8 collective-permute-start.1
  23.3 5.7 %collective-permute-done.2 = bf16[1,128,256]{1,2,0:T(8,128)(2,1)S(1)} collective-permute-done((bf16[1,128,256]{1,2,0:T(8,128)(2,1)S(1)}, bf16[1,128,256]{1,2,0:T(8,128)(2,1)S(1)}, u32[]{:S(2)}, u32[]{:S(2)}) %collective-permute-start.2) | collective-permute-done | bytes 65568 | tf_op jit(solution)/shard_map/while/body/eval_jaxpr/ppermute | solution.py:22
  41.3 9.1 %collective-permute-done = bf16[6,128,256]{1,2,0:T(8,128)(2,1)S(1)} collective-permute-done((bf16[6,128,256]{1,2,0:T(8,128)(2,1)}, bf16[6,128,256]{1,2,0:T(8,128)(2,1)S(1)}, u32[]{:S(2)}, u32[]{:S(2)}) %collective-permute-start) | collective-permute-done | bytes 393248 | tf_op jit(solution)/shard_map/while/body/eval_jaxpr/ppermute | solution.py:12
  50.3 4.2 collective-permute-start.1
  56.5 5.7 %collective-permute-done.2 = bf16[1,128,256]{1,2,0:T(8,128)(2,1)S(1)} collective-permute-done((bf16[1,128,256]{1,2,0:T(8,128)(2,1)S(1)}, bf16[1,128,256]{1,2,0:T(8,128)(2,1)S(1)}, u32[]{:S(2)}, u32[]{:S(2)}) %collective-permute-start.2) | collective-permute-done | bytes 65568 | tf_op jit(solution)/shard_map/while/body/eval_jaxpr/ppermute | solution.py:22
  74.5 9.1 %collective-permute-done = bf16[6,128,256]{1,2,0:T(8,128)(2,1)S(1)} collective-permute-done((bf16[6,128,256]{1,2,0:T(8,128)(2,1)}, bf16[6,128,256]{1,2,0:T(8,128)(2,1)S(1)}, u32[]{:S(2)}, u32[]{:S(2)}) %collective-permute-start) | collective-permute-done | bytes 393248 | tf_op jit(solution)/shard_map/while/body/eval_jaxpr/ppermute | solution.py:12
  83.6 4.3 collective-permute-start.1
  89.8 5.7 %collective-permute-done.2 = bf16[1,128,256]{1,2,0:T(8,128)(2,1)S(1)} collective-permute-done((bf16[1,128,256]{1,2,0:T(8,128)(2,1)S(1)}, bf16[1,128,256]{1,2,0:T(8,128)(2,1)S(1)}, u32[]{:S(2)}, u32[]{:S(2)}) %collective-permute-start.2) | collective-permute-done | bytes 65568 | tf_op jit(solution)/shard_map/while/body/eval_jaxpr/ppermute | solution.py:22
  107.8 9.1 %collective-permute-done = bf16[6,128,256]{1,2,0:T(8,128)(2,1)S(1)} collective-permute-done((bf16[6,128,256]{1,2,0:T(8,128)(2,1)}, bf16[6,128,256]{1,2,0:T(8,128)(2,1)S(1)}, u32[]{:S(2)}, u32[]{:S(2)}) %collective-permute-start) | collective-permute-done | bytes 393248 | tf_op jit(solution)/shard_map/while/body/eval_jaxpr/ppermute | solution.py:12
  116.9 3.7 collective-permute-start.1
  122.6 5.7 %collective-permute-done.2 = bf16[1,128,256]{1,2,0:T(8,128)(2,1)S(1)} collective-permute-done((bf16[1,128,256]{1,2,0:T(8,128)(2,1)S(1)}, bf16[1,128,256]{1,2,0:T(8,128)(2,1)S(1)}, u32[]{:S(2)}, u32[]{:S(2)}) %collective-permute-start.2) | collective-permute-done | bytes 65568 | tf_op jit(solution)/shard_map/while/body/eval_jaxpr/ppermute | solution.py:22
  140.6 9.1 %collective-permute-done = bf16[6,128,256]{1,2,0:T(8,128)(2,1)S(1)} collective-permute-done((bf16[6,128,256]{1,2,0:T(8,128)(2,1)}, bf16[6,128,256]{1,2,0:T(8,128)(2,1)S(1)}, u32[]{:S(2)}, u32[]{:S(2)}) %collective-permute-start) | collective-permute-done | bytes 393248 | tf_op jit(solution)/shard_map/while/body/eval_jaxpr/ppermute | solution.py:12
  149.6 3.5 collective-permute-start.1
  155.0 5.7 %collective-permute-done.2 = bf16[1,128,256]{1,2,0:T(8,128)(2,1)S(1)} collective-permute-done((bf16[1,128,256]{1,2,0:T(8,128)(2,1)S(1)}, bf16[1,128,256]{1,2,0:T(8,128)(2,1)S(1)}, u32[]{:S(2)}, u32[]{:S(2)}) %collective-permute-start.2) | collective-permute-done | bytes 65568 | tf_op jit(solution)/shard_map/while/body/eval_jaxpr/ppermute | solution.py:22
  173.0 9.1 %collective-permute-done = bf16[6,128,256]{1,2,0:T(8,128)(2,1)S(1)} collective-permute-done((bf16[6,128,256]{1,2,0:T(8,128)(2,1)}, bf16[6,128,256]{1,2,0:T(8,128)(2,1)S(1)}, u32[]{:S(2)}, u32[]{:S(2)}) %collective-permute-start) | collective-permute-done | bytes 393248 | tf_op jit(solution)/shard_map/while/body/eval_jaxpr/ppermute | solution.py:12
  182.1 3.1 collective-permute-start.1
  187.2 5.7 %collective-permute-done.2 = bf16[1,128,256]{1,2,0:T(8,128)(2,1)S(1)} collective-permute-done((bf16[1,128,256]{1,2,0:T(8,128)(2,1)S(1)}, bf16[1,128,256]{1,2,0:T(8,128)(2,1)S(1)}, u32[]{:S(2)}, u32[]{:S(2)}) %collective-permute-start.2) | collective-permute-done | bytes 65568 | tf_op jit(solution)/shard_map/while/body/eval_jaxpr/ppermute | solution.py:22
  205.2 9.1 %collective-permute-done = bf16[6,128,256]{1,2,0:T(8,128)(2,1)S(1)} collective-permute-done((bf16[6,128,256]{1,2,0:T(8,128)(2,1)}, bf16[6,128,256]{1,2,0:T(8,128)(2,1)S(1)}, u32[]{:S(2)}, u32[]{:S(2)}) %collective-permute-start) | collective-permute-done | bytes 393248 | tf_op jit(solution)/shard_map/while/body/eval_jaxpr/ppermute | solution.py:12
  214.3 2.8 collective-permute-start.1
  219.0 5.7 %collective-permute-done.2 = bf16[1,128,256]{1,2,0:T(8,128)(2,1)S(1)} collective-permute-done((bf16[1,128,256]{1,2,0:T(8,128)(2,1)S(1)}, bf16[1,128,256]{1,2,0:T(8,128)(2,1)S(1)}, u32[]{:S(2)}, u32[]{:S(2)}) %collective-permute-start.2) | collective-permute-done | bytes 65568 | tf_op jit(solution)/shard_map/while/body/eval_jaxpr/ppermute | solution.py:22
  237.0 9.1 %collective-permute-done = bf16[6,128,256]{1,2,0:T(8,128)(2,1)S(1)} collective-permute-done((bf16[6,128,256]{1,2,0:T(8,128)(2,1)}, bf16[6,128,256]{1,2,0:T(8,128)(2,1)S(1)}, u32[]{:S(2)}, u32[]{:S(2)}) %collective-permute-start) | collective-permute-done | bytes 393248 | tf_op jit(solution)/shard_map/while/body/eval_jaxpr/ppermute | solution.py:12
  250.4 5.7 %collective-permute-done.2 = bf16[1,128,256]{1,2,0:T(8,128)(2,1)S(1)} collective-permute-done((bf16[1,128,256]{1,2,0:T(8,128)(2,1)S(1)}, bf16[1,128,256]{1,2,0:T(8,128)(2,1)S(1)}, u32[]{:S(2)}, u32[]{:S(2)}) %collective-permute-start.2) | collective-permute-done | bytes 65568 | tf_op jit(solution)/shard_map/while/body/eval_jaxpr/ppermute | solution.py:22
  268.4 9.1 %collective-permute-done = bf16[6,128,256]{1,2,0:T(8,128)(2,1)S(1)} collective-permute-done((bf16[6,128,256]{1,2,0:T(8,128)(2,1)}, bf16[6,128,256]{1,2,0:T(8,128)(2,1)S(1)}, u32[]{:S(2)}, u32[]{:S(2)}) %collective-permute-start) | collective-permute-done | bytes 393248 | tf_op jit(solution)/shard_map/while/body/eval_jaxpr/ppermute | solution.py:12
  281.8 5.3 %collective-permute-done.2 = bf16[1,128,256]{1,2,0:T(8,128)(2,1)S(1)} collective-permute-done((bf16[1,128,256]{1,2,0:T(8,128)(2,1)S(1)}, bf16[1,128,256]{1,2,0:T(8,128)(2,1)S(1)}, u32[]{:S(2)}, u32[]{:S(2)}) %collective-permute-start.2) | collective-permute-done | bytes 65568 | tf_op jit(solution)/shard_map/while/body/eval_jaxpr/ppermute | solution.py:22
  299.3 9.1 %collective-permute-done = bf16[6,128,256]{1,2,0:T(8,128)(2,1)S(1)} collective-permute-done((bf16[6,128,256]{1,2,0:T(8,128)(2,1)}, bf16[6,128,256]{1,2,0:T(8,128)(2,1)S(1)}, u32[]{:S(2)}, u32[]{:S(2)}) %collective-permute-start) | collective-permute-done | bytes 393248 | tf_op jit(solution)/shard_map/while/body/eval_jaxpr/ppermute | solution.py:12
  310.4 2.4 collective-permute-start.2
  312.8 5.3 %collective-permute-done.2 = bf16[1,128,256]{1,2,0:T(8,128)(2,1)S(1)} collective-permute-done((bf16[1,128,256]{1,2,0:T(8,128)(2,1)S(1)}, bf16[1,128,256]{1,2,0:T(8,128)(2,1)S(1)}, u32[]{:S(2)}, u32[]{:S(2)}) %collective-permute-start.2) | collective-permute-done | bytes 65568 | tf_op jit(solution)/shard_map/while/body/eval_jaxpr/ppermute | solution.py:22
  330.3 9.1 %collective-permute-done = bf16[6,128,256]{1,2,0:T(8,128)(2,1)S(1)} collective-permute-done((bf16[6,128,256]{1,2,0:T(8,128)(2,1)}, bf16[6,128,256]{1,2,0:T(8,128)(2,1)S(1)}, u32[]{:S(2)}, u32[]{:S(2)}) %collective-permute-start) | collective-permute-done | bytes 393248 | tf_op jit(solution)/shard_map/while/body/eval_jaxpr/ppermute | solution.py:12
  341.3 2.4 collective-permute-start.2
  343.7 5.3 %collective-permute-done.2 = bf16[1,128,256]{1,2,0:T(8,128)(2,1)S(1)} collective-permute-done((bf16[1,128,256]{1,2,0:T(8,128)(2,1)S(1)}, bf16[1,128,256]{1,2,0:T(8,128)(2,1)S(1)}, u32[]{:S(2)}, u32[]{:S(2)}) %collective-permute-start.2) | collective-permute-done | bytes 65568 | tf_op jit(solution)/shard_map/while/body/eval_jaxpr/ppermute | solution.py:22
  361.2 9.1 %collective-permute-done = bf16[6,128,256]{1,2,0:T(8,128)(2,1)S(1)} collective-permute-done((bf16[6,128,256]{1,2,0:T(8,128)(2,1)}, bf16[6,128,256]{1,2,0:T(8,128)(2,1)S(1)}, u32[]{:S(2)}, u32[]{:S(2)}) %collective-permute-start) | collective-permute-done | bytes 393248 | tf_op jit(solution)/shard_map/while/body/eval_jaxpr/ppermute | solution.py:12
  372.2 2.4 collective-permute-start.2
  374.7 5.3 %collective-permute-done.2 = bf16[1,128,256]{1,2,0:T(8,128)(2,1)S(1)} collective-permute-done((bf16[1,128,256]{1,2,0:T(8,128)(2,1)S(1)}, bf16[1,128,256]{1,2,0:T(8,128)(2,1)S(1)}, u32[]{:S(2)}, u32[]{:S(2)}) %collective-permute-start.2) | collective-permute-done | bytes 65568 | tf_op jit(solution)/shard_map/while/body/eval_jaxpr/ppermute | solution.py:22
  392.2 9.1 %collective-permute-done = bf16[6,128,256]{1,2,0:T(8,128)(2,1)S(1)} collective-permute-done((bf16[6,128,256]{1,2,0:T(8,128)(2,1)}, bf16[6,128,256]{1,2,0:T(8,128)(2,1)S(1)}, u32[]{:S(2)}, u32[]{:S(2)}) %collective-permute-start) | collective-permute-done | bytes 393248 | tf_op jit(solution)/shard_map/while/body/eval_jaxpr/ppermute | solution.py:12
  403.2 2.4 collective-permute-start.2
  405.6 5.3 %collective-permute-done.2 = bf16[1,128,256]{1,2,0:T(8,128)(2,1)S(1)} collective-permute-done((bf16[1,128,256]{1,2,0:T(8,128)(2,1)S(1)}, bf16[1,128,256]{1,2,0:T(8,128)(2,1)S(1)}, u32[]{:S(2)}, u32[]{:S(2)}) %collective-permute-start.2) | collective-permute-done | bytes 65568 | tf_op jit(solution)/shard_map/while/body/eval_jaxpr/ppermute | solution.py:22
  423.1 9.1 %collective-permute-done = bf16[6,128,256]{1,2,0:T(8,128)(2,1)S(1)} collective-permute-done((bf16[6,128,256]{1,2,0:T(8,128)(2,1)}, bf16[6,128,256]{1,2,0:T(8,128)(2,1)S(1)}, u32[]{:S(2)}, u32[]{:S(2)}) %collective-permute-start) | collective-permute-done | bytes 393248 | tf_op jit(solution)/shard_map/while/body/eval_jaxpr/ppermute | solution.py:12
  434.1 2.4 collective-permute-start.2
  436.5 5.3 %collective-permute-done.2 = bf16[1,128,256]{1,2,0:T(8,128)(2,1)S(1)} collective-permute-done((bf16[1,128,256]{1,2,0:T(8,128)(2,1)S(1)}, bf16[1,128,256]{1,2,0:T(8,128)(2,1)S(1)}, u32[]{:S(2)}, u32[]{:S(2)}) %collective-permute-start.2) | collective-permute-done | bytes 65568 | tf_op jit(solution)/shard_map/while/body/eval_jaxpr/ppermute | solution.py:22
  454.0 9.1 %collective-permute-done = bf16[6,128,256]{1,2,0:T(8,128)(2,1)S(1)} collective-permute-done((bf16[6,128,256]{1,2,0:T(8,128)(2,1)}, bf16[6,128,256]{1,2,0:T(8,128)(2,1)S(1)}, u32[]{:S(2)}, u32[]{:S(2)}) %collective-permute-start) | collective-permute-done | bytes 393248 | tf_op jit(solution)/shard_map/while/body/eval_jaxpr/ppermute | solution.py:12
  465.0 2.4 collective-permute-start.2
  467.5 5.3 %collective-permute-done.2 = bf16[1,128,256]{1,2,0:T(8,128)(2,1)S(1)} collective-permute-done((bf16[1,128,256]{1,2,0:T(8,128)(2,1)S(1)}, bf16[1,128,256]{1,2,0:T(8,128)(2,1)S(1)}, u32[]{:S(2)}, u32[]{:S(2)}) %collective-permute-start.2) | collective-permute-done | bytes 65568 | tf_op jit(solution)/shard_map/while/body/eval_jaxpr/ppermute | solution.py:22
  485.0 9.1 %collective-permute-done = bf16[6,128,256]{1,2,0:T(8,128)(2,1)S(1)} collective-permute-done((bf16[6,128,256]{1,2,0:T(8,128)(2,1)}, bf16[6,128,256]{1,2,0:T(8,128)(2,1)S(1)}, u32[]{:S(2)}, u32[]{:S(2)}) %collective-permute-start) | collective-permute-done | bytes 393248 | tf_op jit(solution)/shard_map/while/body/eval_jaxpr/ppermute | solution.py:12
  496.0 2.4 collective-permute-start.2
  498.4 5.3 %collective-permute-done.2 = bf16[1,128,256]{1,2,0:T(8,128)(2,1)S(1)} collective-permute-done((bf16[1,128,256]{1,2,0:T(8,128)(2,1)S(1)}, bf16[1,128,256]{1,2,0:T(8,128)(2,1)S(1)}, u32[]{:S(2)}, u32[]{:S(2)}) %collective-permute-start.2) | collective-permute-done | bytes 65568 | tf_op jit(solution)/shard_map/while/body/eval_jaxpr/ppermute | solution.py:22
  (501 shorter events, 232.8 us)
Async XLA Ops:
  3.4 14.2 %collective-permute-start = (bf16[6,128,256]{1,2,0:T(8,128)(2,1)}, bf16[6,128,256]{1,2,0:T(8,128)(2,1)S(1)}, u32[]{:S(2)}, u32[]{:S(2)}) collective-permute-start(bf16[6,128,256]{1,2,0:T(8,128)(2,1)} %get-tuple-element.159), channel_id=1, source_target_pairs={{0,32},{32,64},{64,96},{96,128},{128,160},{160,192},{192,224},{224... | collective-permute-start | bytes 1179656 | tf_op jit(solution)/shard_map/while/body/eval_jaxpr/ppermute | solution.py:12
  17.6 5.7 %collective-permute-start.1 = (bf16[1,128,256]{1,2,0:T(8,128)(2,1)S(1)}, bf16[1,128,256]{1,2,0:T(8,128)(2,1)S(1)}, u32[]{:S(2)}, u32[]{:S(2)}) collective-permute-start(bf16[1,128,256]{1,2,0:T(8,128)(2,1)S(1)} %get-tuple-element.138), channel_id=1, source_target_pairs={{1,0},{2,1},{3,2},{4,3},{5,4},{6,5},{7,6},{8,7},{9,8},{10,9},{11,1... | collective-permute-start | bytes 196616 | tf_op jit(solution)/shard_map/while/body/eval_jaxpr/ppermute | solution.py:23
  21.3 7.7 %collective-permute-start.2 = (bf16[1,128,256]{1,2,0:T(8,128)(2,1)S(1)}, bf16[1,128,256]{1,2,0:T(8,128)(2,1)S(1)}, u32[]{:S(2)}, u32[]{:S(2)}) collective-permute-start(bf16[1,128,256]{1,2,0:T(8,128)(2,1)S(1)} %get-tuple-element.139), channel_id=1, source_target_pairs={{0,1},{1,2},{2,3},{3,4},{4,5},{5,6},{6,7},{7,8},{8,9},{9,10},{10,1... | collective-permute-start | bytes 196616 | tf_op jit(solution)/shard_map/while/body/eval_jaxpr/ppermute | solution.py:22
  39.2 11.1 %collective-permute-start = (bf16[6,128,256]{1,2,0:T(8,128)(2,1)}, bf16[6,128,256]{1,2,0:T(8,128)(2,1)S(1)}, u32[]{:S(2)}, u32[]{:S(2)}) collective-permute-start(bf16[6,128,256]{1,2,0:T(8,128)(2,1)} %get-tuple-element.159), channel_id=1, source_target_pairs={{0,32},{32,64},{64,96},{96,128},{128,160},{160,192},{192,224},{224... | collective-permute-start | bytes 1179656 | tf_op jit(solution)/shard_map/while/body/eval_jaxpr/ppermute | solution.py:12
  50.3 6.2 %collective-permute-start.1 = (bf16[1,128,256]{1,2,0:T(8,128)(2,1)S(1)}, bf16[1,128,256]{1,2,0:T(8,128)(2,1)S(1)}, u32[]{:S(2)}, u32[]{:S(2)}) collective-permute-start(bf16[1,128,256]{1,2,0:T(8,128)(2,1)S(1)} %get-tuple-element.138), channel_id=1, source_target_pairs={{1,0},{2,1},{3,2},{4,3},{5,4},{6,5},{7,6},{8,7},{9,8},{10,9},{11,1... | collective-permute-start | bytes 196616 | tf_op jit(solution)/shard_map/while/body/eval_jaxpr/ppermute | solution.py:23
  54.6 7.7 %collective-permute-start.2 = (bf16[1,128,256]{1,2,0:T(8,128)(2,1)S(1)}, bf16[1,128,256]{1,2,0:T(8,128)(2,1)S(1)}, u32[]{:S(2)}, u32[]{:S(2)}) collective-permute-start(bf16[1,128,256]{1,2,0:T(8,128)(2,1)S(1)} %get-tuple-element.139), channel_id=1, source_target_pairs={{0,1},{1,2},{2,3},{3,4},{4,5},{5,6},{6,7},{7,8},{8,9},{9,10},{10,1... | collective-permute-start | bytes 196616 | tf_op jit(solution)/shard_map/while/body/eval_jaxpr/ppermute | solution.py:22
  72.5 11.1 %collective-permute-start = (bf16[6,128,256]{1,2,0:T(8,128)(2,1)}, bf16[6,128,256]{1,2,0:T(8,128)(2,1)S(1)}, u32[]{:S(2)}, u32[]{:S(2)}) collective-permute-start(bf16[6,128,256]{1,2,0:T(8,128)(2,1)} %get-tuple-element.159), channel_id=1, source_target_pairs={{0,32},{32,64},{64,96},{96,128},{128,160},{160,192},{192,224},{224... | collective-permute-start | bytes 1179656 | tf_op jit(solution)/shard_map/while/body/eval_jaxpr/ppermute | solution.py:12
  83.6 6.2 %collective-permute-start.1 = (bf16[1,128,256]{1,2,0:T(8,128)(2,1)S(1)}, bf16[1,128,256]{1,2,0:T(8,128)(2,1)S(1)}, u32[]{:S(2)}, u32[]{:S(2)}) collective-permute-start(bf16[1,128,256]{1,2,0:T(8,128)(2,1)S(1)} %get-tuple-element.138), channel_id=1, source_target_pairs={{1,0},{2,1},{3,2},{4,3},{5,4},{6,5},{7,6},{8,7},{9,8},{10,9},{11,1... | collective-permute-start | bytes 196616 | tf_op jit(solution)/shard_map/while/body/eval_jaxpr/ppermute | solution.py:23
  87.9 7.7 %collective-permute-start.2 = (bf16[1,128,256]{1,2,0:T(8,128)(2,1)S(1)}, bf16[1,128,256]{1,2,0:T(8,128)(2,1)S(1)}, u32[]{:S(2)}, u32[]{:S(2)}) collective-permute-start(bf16[1,128,256]{1,2,0:T(8,128)(2,1)S(1)} %get-tuple-element.139), channel_id=1, source_target_pairs={{0,1},{1,2},{2,3},{3,4},{4,5},{5,6},{6,7},{7,8},{8,9},{9,10},{10,1... | collective-permute-start | bytes 196616 | tf_op jit(solution)/shard_map/while/body/eval_jaxpr/ppermute | solution.py:22
  105.8 11.1 %collective-permute-start = (bf16[6,128,256]{1,2,0:T(8,128)(2,1)}, bf16[6,128,256]{1,2,0:T(8,128)(2,1)S(1)}, u32[]{:S(2)}, u32[]{:S(2)}) collective-permute-start(bf16[6,128,256]{1,2,0:T(8,128)(2,1)} %get-tuple-element.159), channel_id=1, source_target_pairs={{0,32},{32,64},{64,96},{96,128},{128,160},{160,192},{192,224},{224... | collective-permute-start | bytes 1179656 | tf_op jit(solution)/shard_map/while/body/eval_jaxpr/ppermute | solution.py:12
  116.9 5.7 %collective-permute-start.1 = (bf16[1,128,256]{1,2,0:T(8,128)(2,1)S(1)}, bf16[1,128,256]{1,2,0:T(8,128)(2,1)S(1)}, u32[]{:S(2)}, u32[]{:S(2)}) collective-permute-start(bf16[1,128,256]{1,2,0:T(8,128)(2,1)S(1)} %get-tuple-element.138), channel_id=1, source_target_pairs={{1,0},{2,1},{3,2},{4,3},{5,4},{6,5},{7,6},{8,7},{9,8},{10,9},{11,1... | collective-permute-start | bytes 196616 | tf_op jit(solution)/shard_map/while/body/eval_jaxpr/ppermute | solution.py:23
  120.6 7.7 %collective-permute-start.2 = (bf16[1,128,256]{1,2,0:T(8,128)(2,1)S(1)}, bf16[1,128,256]{1,2,0:T(8,128)(2,1)S(1)}, u32[]{:S(2)}, u32[]{:S(2)}) collective-permute-start(bf16[1,128,256]{1,2,0:T(8,128)(2,1)S(1)} %get-tuple-element.139), channel_id=1, source_target_pairs={{0,1},{1,2},{2,3},{3,4},{4,5},{5,6},{6,7},{7,8},{8,9},{9,10},{10,1... | collective-permute-start | bytes 196616 | tf_op jit(solution)/shard_map/while/body/eval_jaxpr/ppermute | solution.py:22
  138.5 11.1 %collective-permute-start = (bf16[6,128,256]{1,2,0:T(8,128)(2,1)}, bf16[6,128,256]{1,2,0:T(8,128)(2,1)S(1)}, u32[]{:S(2)}, u32[]{:S(2)}) collective-permute-start(bf16[6,128,256]{1,2,0:T(8,128)(2,1)} %get-tuple-element.159), channel_id=1, source_target_pairs={{0,32},{32,64},{64,96},{96,128},{128,160},{160,192},{192,224},{224... | collective-permute-start | bytes 1179656 | tf_op jit(solution)/shard_map/while/body/eval_jaxpr/ppermute | solution.py:12
  149.6 5.4 %collective-permute-start.1 = (bf16[1,128,256]{1,2,0:T(8,128)(2,1)S(1)}, bf16[1,128,256]{1,2,0:T(8,128)(2,1)S(1)}, u32[]{:S(2)}, u32[]{:S(2)}) collective-permute-start(bf16[1,128,256]{1,2,0:T(8,128)(2,1)S(1)} %get-tuple-element.138), channel_id=1, source_target_pairs={{1,0},{2,1},{3,2},{4,3},{5,4},{6,5},{7,6},{8,7},{9,8},{10,9},{11,1... | collective-permute-start | bytes 196616 | tf_op jit(solution)/shard_map/while/body/eval_jaxpr/ppermute | solution.py:23
  153.1 7.7 %collective-permute-start.2 = (bf16[1,128,256]{1,2,0:T(8,128)(2,1)S(1)}, bf16[1,128,256]{1,2,0:T(8,128)(2,1)S(1)}, u32[]{:S(2)}, u32[]{:S(2)}) collective-permute-start(bf16[1,128,256]{1,2,0:T(8,128)(2,1)S(1)} %get-tuple-element.139), channel_id=1, source_target_pairs={{0,1},{1,2},{2,3},{3,4},{4,5},{5,6},{6,7},{7,8},{8,9},{9,10},{10,1... | collective-permute-start | bytes 196616 | tf_op jit(solution)/shard_map/while/body/eval_jaxpr/ppermute | solution.py:22
  171.0 11.1 %collective-permute-start = (bf16[6,128,256]{1,2,0:T(8,128)(2,1)}, bf16[6,128,256]{1,2,0:T(8,128)(2,1)S(1)}, u32[]{:S(2)}, u32[]{:S(2)}) collective-permute-start(bf16[6,128,256]{1,2,0:T(8,128)(2,1)} %get-tuple-element.159), channel_id=1, source_target_pairs={{0,32},{32,64},{64,96},{96,128},{128,160},{160,192},{192,224},{224... | collective-permute-start | bytes 1179656 | tf_op jit(solution)/shard_map/while/body/eval_jaxpr/ppermute | solution.py:12
  182.1 5.1 collective-permute-start.1
  185.2 7.7 %collective-permute-start.2 = (bf16[1,128,256]{1,2,0:T(8,128)(2,1)S(1)}, bf16[1,128,256]{1,2,0:T(8,128)(2,1)S(1)}, u32[]{:S(2)}, u32[]{:S(2)}) collective-permute-start(bf16[1,128,256]{1,2,0:T(8,128)(2,1)S(1)} %get-tuple-element.139), channel_id=1, source_target_pairs={{0,1},{1,2},{2,3},{3,4},{4,5},{5,6},{6,7},{7,8},{8,9},{9,10},{10,1... | collective-permute-start | bytes 196616 | tf_op jit(solution)/shard_map/while/body/eval_jaxpr/ppermute | solution.py:22
  203.2 11.1 %collective-permute-start = (bf16[6,128,256]{1,2,0:T(8,128)(2,1)}, bf16[6,128,256]{1,2,0:T(8,128)(2,1)S(1)}, u32[]{:S(2)}, u32[]{:S(2)}) collective-permute-start(bf16[6,128,256]{1,2,0:T(8,128)(2,1)} %get-tuple-element.159), channel_id=1, source_target_pairs={{0,32},{32,64},{64,96},{96,128},{128,160},{160,192},{192,224},{224... | collective-permute-start | bytes 1179656 | tf_op jit(solution)/shard_map/while/body/eval_jaxpr/ppermute | solution.py:12
  214.3 4.7 collective-permute-start.1
  217.0 7.7 %collective-permute-start.2 = (bf16[1,128,256]{1,2,0:T(8,128)(2,1)S(1)}, bf16[1,128,256]{1,2,0:T(8,128)(2,1)S(1)}, u32[]{:S(2)}, u32[]{:S(2)}) collective-permute-start(bf16[1,128,256]{1,2,0:T(8,128)(2,1)S(1)} %get-tuple-element.139), channel_id=1, source_target_pairs={{0,1},{1,2},{2,3},{3,4},{4,5},{5,6},{6,7},{7,8},{8,9},{9,10},{10,1... | collective-permute-start | bytes 196616 | tf_op jit(solution)/shard_map/while/body/eval_jaxpr/ppermute | solution.py:22
  235.0 11.1 %collective-permute-start = (bf16[6,128,256]{1,2,0:T(8,128)(2,1)}, bf16[6,128,256]{1,2,0:T(8,128)(2,1)S(1)}, u32[]{:S(2)}, u32[]{:S(2)}) collective-permute-start(bf16[6,128,256]{1,2,0:T(8,128)(2,1)} %get-tuple-element.159), channel_id=1, source_target_pairs={{0,32},{32,64},{64,96},{96,128},{128,160},{160,192},{192,224},{224... | collective-permute-start | bytes 1179656 | tf_op jit(solution)/shard_map/while/body/eval_jaxpr/ppermute | solution.py:12
  246.0 4.4 collective-permute-start.1
  248.4 7.7 %collective-permute-start.2 = (bf16[1,128,256]{1,2,0:T(8,128)(2,1)S(1)}, bf16[1,128,256]{1,2,0:T(8,128)(2,1)S(1)}, u32[]{:S(2)}, u32[]{:S(2)}) collective-permute-start(bf16[1,128,256]{1,2,0:T(8,128)(2,1)S(1)} %get-tuple-element.139), channel_id=1, source_target_pairs={{0,1},{1,2},{2,3},{3,4},{4,5},{5,6},{6,7},{7,8},{8,9},{9,10},{10,1... | collective-permute-start | bytes 196616 | tf_op jit(solution)/shard_map/while/body/eval_jaxpr/ppermute | solution.py:22
  266.3 11.1 %collective-permute-start = (bf16[6,128,256]{1,2,0:T(8,128)(2,1)}, bf16[6,128,256]{1,2,0:T(8,128)(2,1)S(1)}, u32[]{:S(2)}, u32[]{:S(2)}) collective-permute-start(bf16[6,128,256]{1,2,0:T(8,128)(2,1)} %get-tuple-element.159), channel_id=1, source_target_pairs={{0,32},{32,64},{64,96},{96,128},{128,160},{160,192},{192,224},{224... | collective-permute-start | bytes 1179656 | tf_op jit(solution)/shard_map/while/body/eval_jaxpr/ppermute | solution.py:12
  277.4 4.4 collective-permute-start.1
  279.4 7.7 %collective-permute-start.2 = (bf16[1,128,256]{1,2,0:T(8,128)(2,1)S(1)}, bf16[1,128,256]{1,2,0:T(8,128)(2,1)S(1)}, u32[]{:S(2)}, u32[]{:S(2)}) collective-permute-start(bf16[1,128,256]{1,2,0:T(8,128)(2,1)S(1)} %get-tuple-element.139), channel_id=1, source_target_pairs={{0,1},{1,2},{2,3},{3,4},{4,5},{5,6},{6,7},{7,8},{8,9},{9,10},{10,1... | collective-permute-start | bytes 196616 | tf_op jit(solution)/shard_map/while/body/eval_jaxpr/ppermute | solution.py:22
  297.3 11.1 %collective-permute-start = (bf16[6,128,256]{1,2,0:T(8,128)(2,1)}, bf16[6,128,256]{1,2,0:T(8,128)(2,1)S(1)}, u32[]{:S(2)}, u32[]{:S(2)}) collective-permute-start(bf16[6,128,256]{1,2,0:T(8,128)(2,1)} %get-tuple-element.159), channel_id=1, source_target_pairs={{0,32},{32,64},{64,96},{96,128},{128,160},{160,192},{192,224},{224... | collective-permute-start | bytes 1179656 | tf_op jit(solution)/shard_map/while/body/eval_jaxpr/ppermute | solution.py:12
  308.4 4.4 collective-permute-start.1
  310.4 7.7 %collective-permute-start.2 = (bf16[1,128,256]{1,2,0:T(8,128)(2,1)S(1)}, bf16[1,128,256]{1,2,0:T(8,128)(2,1)S(1)}, u32[]{:S(2)}, u32[]{:S(2)}) collective-permute-start(bf16[1,128,256]{1,2,0:T(8,128)(2,1)S(1)} %get-tuple-element.139), channel_id=1, source_target_pairs={{0,1},{1,2},{2,3},{3,4},{4,5},{5,6},{6,7},{7,8},{8,9},{9,10},{10,1... | collective-permute-start | bytes 196616 | tf_op jit(solution)/shard_map/while/body/eval_jaxpr/ppermute | solution.py:22
  328.3 11.1 %collective-permute-start = (bf16[6,128,256]{1,2,0:T(8,128)(2,1)}, bf16[6,128,256]{1,2,0:T(8,128)(2,1)S(1)}, u32[]{:S(2)}, u32[]{:S(2)}) collective-permute-start(bf16[6,128,256]{1,2,0:T(8,128)(2,1)} %get-tuple-element.159), channel_id=1, source_target_pairs={{0,32},{32,64},{64,96},{96,128},{128,160},{160,192},{192,224},{224... | collective-permute-start | bytes 1179656 | tf_op jit(solution)/shard_map/while/body/eval_jaxpr/ppermute | solution.py:12
  339.4 4.4 collective-permute-start.1
  341.3 7.7 %collective-permute-start.2 = (bf16[1,128,256]{1,2,0:T(8,128)(2,1)S(1)}, bf16[1,128,256]{1,2,0:T(8,128)(2,1)S(1)}, u32[]{:S(2)}, u32[]{:S(2)}) collective-permute-start(bf16[1,128,256]{1,2,0:T(8,128)(2,1)S(1)} %get-tuple-element.139), channel_id=1, source_target_pairs={{0,1},{1,2},{2,3},{3,4},{4,5},{5,6},{6,7},{7,8},{8,9},{9,10},{10,1... | collective-permute-start | bytes 196616 | tf_op jit(solution)/shard_map/while/body/eval_jaxpr/ppermute | solution.py:22
  359.2 11.1 %collective-permute-start = (bf16[6,128,256]{1,2,0:T(8,128)(2,1)}, bf16[6,128,256]{1,2,0:T(8,128)(2,1)S(1)}, u32[]{:S(2)}, u32[]{:S(2)}) collective-permute-start(bf16[6,128,256]{1,2,0:T(8,128)(2,1)} %get-tuple-element.159), channel_id=1, source_target_pairs={{0,32},{32,64},{64,96},{96,128},{128,160},{160,192},{192,224},{224... | collective-permute-start | bytes 1179656 | tf_op jit(solution)/shard_map/while/body/eval_jaxpr/ppermute | solution.py:12
  370.3 4.4 collective-permute-start.1
  372.2 7.7 %collective-permute-start.2 = (bf16[1,128,256]{1,2,0:T(8,128)(2,1)S(1)}, bf16[1,128,256]{1,2,0:T(8,128)(2,1)S(1)}, u32[]{:S(2)}, u32[]{:S(2)}) collective-permute-start(bf16[1,128,256]{1,2,0:T(8,128)(2,1)S(1)} %get-tuple-element.139), channel_id=1, source_target_pairs={{0,1},{1,2},{2,3},{3,4},{4,5},{5,6},{6,7},{7,8},{8,9},{9,10},{10,1... | collective-permute-start | bytes 196616 | tf_op jit(solution)/shard_map/while/body/eval_jaxpr/ppermute | solution.py:22
  390.1 11.1 %collective-permute-start = (bf16[6,128,256]{1,2,0:T(8,128)(2,1)}, bf16[6,128,256]{1,2,0:T(8,128)(2,1)S(1)}, u32[]{:S(2)}, u32[]{:S(2)}) collective-permute-start(bf16[6,128,256]{1,2,0:T(8,128)(2,1)} %get-tuple-element.159), channel_id=1, source_target_pairs={{0,32},{32,64},{64,96},{96,128},{128,160},{160,192},{192,224},{224... | collective-permute-start | bytes 1179656 | tf_op jit(solution)/shard_map/while/body/eval_jaxpr/ppermute | solution.py:12
  401.2 4.4 collective-permute-start.1
  403.2 7.7 %collective-permute-start.2 = (bf16[1,128,256]{1,2,0:T(8,128)(2,1)S(1)}, bf16[1,128,256]{1,2,0:T(8,128)(2,1)S(1)}, u32[]{:S(2)}, u32[]{:S(2)}) collective-permute-start(bf16[1,128,256]{1,2,0:T(8,128)(2,1)S(1)} %get-tuple-element.139), channel_id=1, source_target_pairs={{0,1},{1,2},{2,3},{3,4},{4,5},{5,6},{6,7},{7,8},{8,9},{9,10},{10,1... | collective-permute-start | bytes 196616 | tf_op jit(solution)/shard_map/while/body/eval_jaxpr/ppermute | solution.py:22
  421.1 11.1 %collective-permute-start = (bf16[6,128,256]{1,2,0:T(8,128)(2,1)}, bf16[6,128,256]{1,2,0:T(8,128)(2,1)S(1)}, u32[]{:S(2)}, u32[]{:S(2)}) collective-permute-start(bf16[6,128,256]{1,2,0:T(8,128)(2,1)} %get-tuple-element.159), channel_id=1, source_target_pairs={{0,32},{32,64},{64,96},{96,128},{128,160},{160,192},{192,224},{224... | collective-permute-start | bytes 1179656 | tf_op jit(solution)/shard_map/while/body/eval_jaxpr/ppermute | solution.py:12
  432.2 4.4 collective-permute-start.1
  434.1 7.7 %collective-permute-start.2 = (bf16[1,128,256]{1,2,0:T(8,128)(2,1)S(1)}, bf16[1,128,256]{1,2,0:T(8,128)(2,1)S(1)}, u32[]{:S(2)}, u32[]{:S(2)}) collective-permute-start(bf16[1,128,256]{1,2,0:T(8,128)(2,1)S(1)} %get-tuple-element.139), channel_id=1, source_target_pairs={{0,1},{1,2},{2,3},{3,4},{4,5},{5,6},{6,7},{7,8},{8,9},{9,10},{10,1... | collective-permute-start | bytes 196616 | tf_op jit(solution)/shard_map/while/body/eval_jaxpr/ppermute | solution.py:22
  452.0 11.1 %collective-permute-start = (bf16[6,128,256]{1,2,0:T(8,128)(2,1)}, bf16[6,128,256]{1,2,0:T(8,128)(2,1)S(1)}, u32[]{:S(2)}, u32[]{:S(2)}) collective-permute-start(bf16[6,128,256]{1,2,0:T(8,128)(2,1)} %get-tuple-element.159), channel_id=1, source_target_pairs={{0,32},{32,64},{64,96},{96,128},{128,160},{160,192},{192,224},{224... | collective-permute-start | bytes 1179656 | tf_op jit(solution)/shard_map/while/body/eval_jaxpr/ppermute | solution.py:12
  463.1 4.4 collective-permute-start.1
  465.0 7.7 %collective-permute-start.2 = (bf16[1,128,256]{1,2,0:T(8,128)(2,1)S(1)}, bf16[1,128,256]{1,2,0:T(8,128)(2,1)S(1)}, u32[]{:S(2)}, u32[]{:S(2)}) collective-permute-start(bf16[1,128,256]{1,2,0:T(8,128)(2,1)S(1)} %get-tuple-element.139), channel_id=1, source_target_pairs={{0,1},{1,2},{2,3},{3,4},{4,5},{5,6},{6,7},{7,8},{8,9},{9,10},{10,1... | collective-permute-start | bytes 196616 | tf_op jit(solution)/shard_map/while/body/eval_jaxpr/ppermute | solution.py:22
  483.0 11.1 %collective-permute-start = (bf16[6,128,256]{1,2,0:T(8,128)(2,1)}, bf16[6,128,256]{1,2,0:T(8,128)(2,1)S(1)}, u32[]{:S(2)}, u32[]{:S(2)}) collective-permute-start(bf16[6,128,256]{1,2,0:T(8,128)(2,1)} %get-tuple-element.159), channel_id=1, source_target_pairs={{0,32},{32,64},{64,96},{96,128},{128,160},{160,192},{192,224},{224... | collective-permute-start | bytes 1179656 | tf_op jit(solution)/shard_map/while/body/eval_jaxpr/ppermute | solution.py:12
  494.1 4.4 collective-permute-start.1
  496.0 7.7 %collective-permute-start.2 = (bf16[1,128,256]{1,2,0:T(8,128)(2,1)S(1)}, bf16[1,128,256]{1,2,0:T(8,128)(2,1)S(1)}, u32[]{:S(2)}, u32[]{:S(2)}) collective-permute-start(bf16[1,128,256]{1,2,0:T(8,128)(2,1)S(1)} %get-tuple-element.139), channel_id=1, source_target_pairs={{0,1},{1,2},{2,3},{3,4},{4,5},{5,6},{6,7},{7,8},{8,9},{9,10},{10,1... | collective-permute-start | bytes 196616 | tf_op jit(solution)/shard_map/while/body/eval_jaxpr/ppermute | solution.py:22
  (32 other events, 80.2 us)
where the time goes:
time: 518 us; the launch traced here: 516 us
  waiting for transfers between devices  235 us (45%)
  matrix products  145 us (28%)
  starting transfers between devices  109 us (21%)
  local copies, waits for them, and re-layouts  21 us (4%)
    ppermute x16, waiting for transfers between devices, shifted(): return lax.ppermute(block, axis, route)  147 us
    ppermute x16, waiting for transfers between devices, with_halo(): before = lax.ppermute(last, axis, up)  88 us
    dot_general x96, matrix products, supernode(): jnp.dot(inverses[a], residue.astype(jnp.bfloat16), preferred_element_type...  87 us
    ppermute x16, starting transfers between devices, with_halo(): after = lax.ppermute(initial, axis, down)  43.1 us
    ppermute x16, starting transfers between devices, with_halo(): before = lax.ppermute(last, axis, up)  34.6 us
    dot_general x16, matrix products, supernode(): lax.dot_general(coupling, picked, (((1, 3), (1, 2)), ((0,), (0,))), prefe...  33.3 us
    ppermute x16, starting transfers between devices, shifted(): return lax.ppermute(block, axis, route)  31.5 us
    dot_general x160, matrix products, supernode(): jnp.dot(supernode_blocks[a * (a - 1) // 2 + b], solved[b], preferred_elem...  25.2 us
  transfers between devices with their start and end apart: 48, of which 32 were waited for; matrix products, arithmetic and copies ran while one was open for 0% of the time, Pallas kernels for 0%

commit v1 on v0

v1 whole, which is shorter than its diff:
```python
import functools

import jax
import jax.numpy as jnp
from jax import lax
from jax.experimental import pallas as pl
from jax.experimental.pallas import tpu as pltpu
from jax.sharding import PartitionSpec as P

BLK = 128
BD = 6
NNZ = 5
WIN = BD + 2
CHUNKS = (128, 128)
PERIOD = 6
NT = (((1,), (1,)), ((), ()))


def dot_nt(x, y):
    return lax.dot_general(x, y, NT, preferred_element_type=jnp.float32)


def load(pairs, sems):
    copies = [pltpu.make_async_copy(src, dst, sems.at[i]) for i, (src, dst) in enumerate(pairs)]
    for copy in copies:
        copy.start()
    for copy in copies:
        copy.wait()


def substitute(out, known, sup, inv, a):
    if a:
        q = a * (a - 1) // 2
        coefs = jnp.concatenate([sup[q + b] for b in range(a)], axis=1)
        known = known - dot_nt(out[:, : a * BLK], coefs)
    out[:, a * BLK : (a + 1) * BLK] = dot_nt(known.astype(jnp.bfloat16), inv[a]).astype(jnp.bfloat16)


def sides_kernel(rhs_hbm, inv_hbm, sup_hbm, gt, rhs, inv, sup, sems):
    load(((inv_hbm, inv), (rhs_hbm, rhs), (sup_hbm, sup)), sems)
    for a in range(BD):
        substitute(gt, rhs[a].T.astype(jnp.float32), sup, inv, a)


def matrix_kernel(pattern_hbm, inv_hbm, cpl_hbm, sup_hbm, ht, ct, pattern, inv, cpl, sup, sems):
    load(((pattern_hbm, pattern), (inv_hbm, inv), (sup_hbm, sup), (cpl_hbm, cpl)), sems)
    first = lax.axis_index("row") * BD - 1
    for a in range(BD):
        ct[...] = jnp.zeros_like(ct)

        @pl.when(lax.axis_index("sec") > 0)
        def _():
            for n in range(NNZ):
                at = jnp.clip(pattern[a, n] - first, 0, WIN - 1)
                ct[pl.ds(pl.multiple_of(at * BLK, BLK), BLK), :] = cpl[a, n].T

        substitute(ht, ct[...].astype(jnp.float32), sup, inv, a)


def settle_kernel(_, kept):
    pass


def step_kernel(tick, rows, last, matrix, *refs):
    if last:
        *arrived, ht, _, gt = refs
    else:
        *arrived, ht, _, own, cross, mate, gt = refs if matrix else (*refs[:1], *refs)
    odd = lax.rem(lax.axis_index("row"), 2) == 1

    def emit(value):
        own[...] = value
        first, final = value[:, :BLK], value[:, (BD - 1) * BLK :]
        cross[...] = jnp.where(odd, final, first)
        mate[...] = jnp.where(odd, first, final)

    @pl.when(lax.axis_index("sec") == tick)
    def _():
        if not arrived:
            emit(gt[rows, :])
        else:
            main, cross_in, mate_in = (ref[...] for ref in arrived)
            low = jnp.where(odd, mate_in, cross_in)
            high = jnp.where(odd, cross_in, mate_in)
            window = jnp.concatenate([low, main, high], axis=1)
            update = jnp.dot(window, ht[...], preferred_element_type=jnp.float32)
            value = (gt[rows, :].astype(jnp.float32) - update).astype(jnp.bfloat16)
            gt[rows, :] = value
            if not last:
                emit(value)


def finish_kernel(gt, out):
    for a in range(BD):
        out[a] = gt[:, a * BLK : (a + 1) * BLK].T


def local(right_sides, inverses, coupling, supernode_blocks, pattern):
    sections = lax.axis_size("sec")
    devices = lax.axis_size("row")
    nrhs = right_sides.shape[2]
    bf16 = jnp.bfloat16
    vmem = pl.BlockSpec(memory_space=pltpu.VMEM)
    params = pltpu.CompilerParams(vmem_limit_bytes=16 * 2**20)

    pattern, right_sides, inverses, coupling, supernode_blocks = (
        pltpu.with_memory_space_constraint(x, pltpu.HBM)
        for x in (pattern, right_sides, inverses, coupling, supernode_blocks)
    )

    def prepared(kernel, rows, operands, scratch, flops, name):
        return pl.pallas_call(
            kernel,
            out_shape=pltpu.VMEM((rows, BD * BLK), bf16),
            in_specs=[pl.BlockSpec(memory_space=pltpu.HBM)] * len(operands),
            out_specs=vmem,
            scratch_shapes=scratch
            + [(pltpu.SMEM if x is pattern else pltpu.VMEM)(x.shape, x.dtype) for x in operands]
            + [pltpu.SemaphoreType.DMA((len(operands),))],
            compiler_params=params,
            cost_estimate=pl.CostEstimate(flops=flops, bytes_accessed=2**21, transcendentals=0),
            name=name,
        )(*operands)

    gt = prepared(sides_kernel, nrhs, (right_sides, inverses, supernode_blocks), [], 2**28, "sides")
    ht = prepared(
        matrix_kernel,
        WIN * BLK,
        (pattern, inverses, coupling, supernode_blocks),
        [pltpu.VMEM((WIN * BLK, BLK), bf16)],
        1_900_000_000,
        "matrix",
    )

    def settled(arrived):
        return pl.pallas_call(
            settle_kernel,
            out_shape=pltpu.VMEM(arrived.shape, bf16),
            in_specs=[vmem],
            out_specs=vmem,
            input_output_aliases={0: 0},
            compiler_params=params,
            cost_estimate=pl.CostEstimate(flops=1, bytes_accessed=0, transcendentals=0),
            name="settle",
        )(arrived)

    def step(tick, start, wide, arrived, gt):
        matrix = bool(arrived) or start > 0
        operands = (*arrived, ht, gt) if matrix else (gt,)
        last = tick == sections - 1
        results = [] if last else [pltpu.VMEM((wide, columns), bf16) for columns in (BD * BLK, BLK, BLK)]
        results.append(pltpu.VMEM((nrhs, BD * BLK), bf16))
        return pl.pallas_call(
            functools.partial(step_kernel, tick, slice(start, start + wide), last, matrix),
            out_shape=results,
            in_specs=[vmem] * len(operands),
            out_specs=[vmem] * len(results),
            input_output_aliases={len(operands) - 1: len(results) - 1},
            compiler_params=params,
            cost_estimate=pl.CostEstimate(flops=1900000000, bytes_accessed=0, transcendentals=0),
            name="step",
        )(*operands)

    def route(tick, target):
        return [
            (s * devices + d, (s + 1) * devices + target(d))
            for s in range(sections - 1)
            for d in range(devices)
            if s % PERIOD == tick % PERIOD and 0 <= target(d) < devices
        ]

    starts = [sum(CHUNKS[:k]) for k in range(len(CHUNKS))]
    arrived = [()] * len(CHUNKS)
    for tick in range(sections):
        for k, (start, wide) in enumerate(zip(starts, CHUNKS)):
            *outgoing, gt = step(tick, start, wide, arrived[k], gt)
            if outgoing:
                own, cross, mate = outgoing
                arrived[k] = (
                    settled(lax.ppermute(own, ("sec", "row"), route(tick, lambda d: d))),
                    lax.ppermute(cross, ("sec", "row"), route(tick, lambda d: d + 1 if d % 2 else d - 1)),
                    lax.ppermute(mate, ("sec", "row"), route(tick, lambda d: d ^ 1)),
                )
    return pl.pallas_call(
        finish_kernel,
        out_shape=jax.ShapeDtypeStruct((BD, BLK, nrhs), bf16),
        in_specs=[vmem],
        out_specs=vmem,
        compiler_params=params,
        name="finish",
    )(gt)


def solution(mesh):
    return jax.shard_map(
        local,
        mesh=mesh,
        in_specs=(
            P(("sec", "row"), None, None),
            P(("sec", "row"), None, None),
            P(("sec", "row"), None, None, None),
            P(("sec", "row"), None, None),
            P(("sec", "row"), None),
        ),
        out_specs=P(("sec", "row"), None, None),
        check_vma=False,
    )
```

time: 518 us -> 154 us (0.30)
  the two profiles are of different devices: /device:TPU:390 before, /device:TPU:482 now
where the time goes in v1:
time: 154 us; the launch traced here: 153 us
  starting transfers between devices  71.2 us (46%)
  waiting for transfers between devices  69.8 us (45%)
  Pallas kernels  10.2 us (7%)
  between operations  1.8 us (1%)
    ppermute x30, waiting for transfers between devices, local(): lax.ppermute(own, ('sec', 'row'), route(tick, lambda d: d))  66.1 us
    ppermute x30, starting transfers between devices, local(): lax.ppermute(own, ('sec', 'row'), route(tick, lambda d: d))  23.9 us
    ppermute x30, starting transfers between devices, local(): lax.ppermute(cross, ('sec', 'row'), route(tick, lambda d: d + 1 if d % 2...  23.7 us
    ppermute x30, starting transfers between devices, local(): lax.ppermute(mate, ('sec', 'row'), route(tick, lambda d: d ^ 1))  23.6 us
    pallas_call x2, Pallas kernels, prepared(): pl.pallas_call(kernel, out_shape=pltpu.VMEM((rows, BD * BLK), bf16), in_s...  8.01 us
    ppermute x30, waiting for transfers between devices, local(): lax.ppermute(cross, ('sec', 'row'), route(tick, lambda d: d + 1 if d % 2...  3.65 us
  transfers between devices with their start and end apart: 90, of which 10 were waited for; matrix products, arithmetic and copies ran while one was open for 0% of the time, Pallas kernels for 4%

profile of v1, /device:TPU:482, one launch (start us, length us, event | category | flops | bytes accessed | tf_op | source)
XLA Modules:
  0.0 153.0 jit_solution(12671585509066900357)
XLA Ops:
  0.0 2.8 %sides.1.refs_0_ = bf16[256,768]{1,0:T(8,128)(2,1)S(1)} custom-call(bf16[6,128,256]{2,1,0:T(8,128)(2,1)} %rhs_hbm.1, bf16[6,128,128]{2,1,0:T(8,128)(2,1)} %inv_hbm.3, bf16[15,128,128]{2,1,0:T(8,128)(2,1)} %sup_hbm.3), custom_call_target="tpu_custom_call" | custom-call | flops 268435456 | bytes 2097152 | tf_op jit(solution)/shard_map/sides/pallas_call | solution.py:112
  4.1 0.7 collective-permute-start.3
  4.8 5.2 %matrix.1.refs_0_.refs_3_ = bf16[1024,768]{1,0:T(8,128)(2,1)S(1)} custom-call(s32[6,5]{1,0:T(8,128)} %pattern_hbm.1, bf16[6,128,128]{2,1,0:T(8,128)(2,1)} %inv_hbm.3, bf16[6,5,128,128]{3,2,1,0:T(8,128)(2,1)} %cpl_hbm.1, bf16[15,128,128]{2,1,0:T(8,128)(2,1)} %sup_hbm.3), custom_call_target="tpu_custom_call" | custom-call | flops 1900000000 | bytes 2097152 | tf_op jit(solution)/shard_map/matrix/pallas_call | solution.py:112
  10.1 0.7 collective-permute-start
  12.2 0.7 collective-permute-start.9
  14.3 0.7 collective-permute-start.6
  16.4 1.3 collective-permute-start.15
  17.7 1.3 collective-permute-start.16
  19.0 1.3 collective-permute-start.17
  20.3 1.3 collective-permute-start.12
  21.6 1.3 collective-permute-start.13
  22.9 11.6 %collective-permute-done.15._ = bf16[128,768]{1,0:T(8,128)(2,1)S(1)} collective-permute-done((bf16[128,768]{1,0:T(8,128)(2,1)S(1)}, bf16[128,768]{1,0:T(8,128)(2,1)S(1)}, u32[]{:S(2)}, u32[]{:S(2)}) %collective-permute-start.15) | collective-permute-done | bytes 196640 | tf_op jit(solution)/shard_map/ppermute | solution.py:180
  34.5 1.3 collective-permute-start.14
  35.9 0.7 collective-permute-start.21
  37.2 3.8 %collective-permute-done.12._ = bf16[128,768]{1,0:T(8,128)(2,1)S(1)} collective-permute-done((bf16[128,768]{1,0:T(8,128)(2,1)S(1)}, bf16[128,768]{1,0:T(8,128)(2,1)S(1)}, u32[]{:S(2)}, u32[]{:S(2)}) %collective-permute-start.12) | collective-permute-done | bytes 196640 | tf_op jit(solution)/shard_map/ppermute | solution.py:180
  41.6 1.1 collective-permute-done.13.refs_1_
  44.8 0.7 collective-permute-start.27
  46.9 0.7 collective-permute-start.24
  48.9 0.7 collective-permute-start.33
  51.0 0.7 collective-permute-start.30
  53.1 0.7 collective-permute-start.39
  55.2 0.7 collective-permute-start.36
  57.3 0.7 collective-permute-start.45
  59.4 0.7 collective-permute-start.42
  61.5 1.3 collective-permute-start.51
  62.8 1.3 collective-permute-start.52
  64.1 1.3 collective-permute-start.53
  65.5 1.3 collective-permute-start.48
  66.8 1.3 collective-permute-start.49
  68.1 21.9 %collective-permute-done.51._ = bf16[128,768]{1,0:T(8,128)(2,1)S(1)} collective-permute-done((bf16[128,768]{1,0:T(8,128)(2,1)S(1)}, bf16[128,768]{1,0:T(8,128)(2,1)S(1)}, u32[]{:S(2)}, u32[]{:S(2)}) %collective-permute-start.51) | collective-permute-done | bytes 196640 | tf_op jit(solution)/shard_map/ppermute | solution.py:180
  90.0 1.3 collective-permute-start.50
  92.9 3.0 %collective-permute-done.48._ = bf16[128,768]{1,0:T(8,128)(2,1)S(1)} collective-permute-done((bf16[128,768]{1,0:T(8,128)(2,1)S(1)}, bf16[128,768]{1,0:T(8,128)(2,1)S(1)}, u32[]{:S(2)}, u32[]{:S(2)}) %collective-permute-start.48) | collective-permute-done | bytes 196640 | tf_op jit(solution)/shard_map/ppermute | solution.py:180
  99.1 0.7 collective-permute-start.63
  105.4 0.7 collective-permute-start.66
  107.5 0.7 collective-permute-start.75
  109.6 0.7 collective-permute-start.72
  111.7 0.7 collective-permute-start.81
  113.8 0.7 collective-permute-start.78
  115.9 1.3 collective-permute-start.88
  117.2 1.3 collective-permute-start.87
  118.5 1.3 collective-permute-start.89
  119.8 1.3 collective-permute-start.84
  121.1 1.3 collective-permute-start.85
  122.4 23.2 %collective-permute-done.87._ = bf16[128,768]{1,0:T(8,128)(2,1)S(1)} collective-permute-done((bf16[128,768]{1,0:T(8,128)(2,1)S(1)}, bf16[128,768]{1,0:T(8,128)(2,1)S(1)}, u32[]{:S(2)}, u32[]{:S(2)}) %collective-permute-start.87) | collective-permute-done | bytes 196640 | tf_op jit(solution)/shard_map/ppermute | solution.py:180
  145.6 1.3 collective-permute-start.86
  147.3 2.6 %collective-permute-done.84._ = bf16[128,768]{1,0:T(8,128)(2,1)S(1)} collective-permute-done((bf16[128,768]{1,0:T(8,128)(2,1)S(1)}, bf16[128,768]{1,0:T(8,128)(2,1)S(1)}, u32[]{:S(2)}, u32[]{:S(2)}) %collective-permute-start.84) | collective-permute-done | bytes 196640 | tf_op jit(solution)/shard_map/ppermute | solution.py:180
  149.9 1.8 %collective-permute-done.85.refs_1_ = bf16[128,128]{1,0:T(8,128)(2,1)S(1)} collective-permute-done((bf16[128,128]{1,0:T(8,128)(2,1)S(1)}, bf16[128,128]{1,0:T(8,128)(2,1)S(1)}, u32[]{:S(2)}, u32[]{:S(2)}) %collective-permute-start.85) | collective-permute-done | bytes 32800 | tf_op jit(solution)/shard_map/ppermute | solution.py:181
  152.1 0.9 finish.1
  (197 shorter events, 37.5 us)
Async XLA Ops:
  2.8 9.3 %collective-permute-start.4 = (bf16[128,128]{1,0:T(8,128)(2,1)S(1)}, bf16[128,128]{1,0:T(8,128)(2,1)S(1)}, u32[]{:S(2)}, u32[]{:S(2)}) collective-permute-start(bf16[128,128]{1,0:T(8,128)(2,1)S(1)} %get-tuple-element.130), channel_id=1, source_target_pairs={{1,34},{2,33},{3,36},{4,35},{5,38},{6,37},{7,40},{8,39},{9,42},{10... | collective-permute-start | bytes 98312 | tf_op jit(solution)/shard_map/ppermute | solution.py:181
  3.5 8.7 %collective-permute-start.5 = (bf16[128,128]{1,0:T(8,128)(2,1)S(1)}, bf16[128,128]{1,0:T(8,128)(2,1)S(1)}, u32[]{:S(2)}, u32[]{:S(2)}) collective-permute-start(bf16[128,128]{1,0:T(8,128)(2,1)S(1)} %get-tuple-element.131), channel_id=1, source_target_pairs={{0,33},{1,32},{2,35},{3,34},{4,37},{5,36},{6,39},{7,38},{8,41},{9,... | collective-permute-start | bytes 98312 | tf_op jit(solution)/shard_map/ppermute | solution.py:182
  4.1 7.3 %collective-permute-start.3 = (bf16[128,768]{1,0:T(8,128)(2,1)S(1)}, bf16[128,768]{1,0:T(8,128)(2,1)S(1)}, u32[]{:S(2)}, u32[]{:S(2)}) collective-permute-start(bf16[128,768]{1,0:T(8,128)(2,1)S(1)} %get-tuple-element.129), channel_id=1, source_target_pairs={{0,32},{1,33},{2,34},{3,35},{4,36},{5,37},{6,38},{7,39},{8,40},{9,... | collective-permute-start | bytes 589832 | tf_op jit(solution)/shard_map/ppermute | solution.py:180
  10.8 3.5 %collective-permute-start.1 = (bf16[128,128]{1,0:T(8,128)(2,1)S(1)}, bf16[128,128]{1,0:T(8,128)(2,1)S(1)}, u32[]{:S(2)}, u32[]{:S(2)}) collective-permute-start(bf16[128,128]{1,0:T(8,128)(2,1)S(1)} %get-tuple-element.127), channel_id=1, source_target_pairs={{1,34},{2,33},{3,36},{4,35},{5,38},{6,37},{7,40},{8,39},{9,42},{10... | collective-permute-start | bytes 98312 | tf_op jit(solution)/shard_map/ppermute | solution.py:181
  12.9 3.5 %collective-permute-start.10 = (bf16[128,128]{1,0:T(8,128)(2,1)S(1)}, bf16[128,128]{1,0:T(8,128)(2,1)S(1)}, u32[]{:S(2)}, u32[]{:S(2)}) collective-permute-start(bf16[128,128]{1,0:T(8,128)(2,1)S(1)} %get-tuple-element.138), channel_id=1, source_target_pairs={{33,66},{34,65},{35,68},{36,67},{37,70},{38,69},{39,72},{40,71},{4... | collective-permute-start | bytes 98312 | tf_op jit(solution)/shard_map/ppermute | solution.py:181
  14.3 4.7 %collective-permute-start.6 = (bf16[128,768]{1,0:T(8,128)(2,1)S(1)}, bf16[128,768]{1,0:T(8,128)(2,1)S(1)}, u32[]{:S(2)}, u32[]{:S(2)}) collective-permute-start(bf16[128,768]{1,0:T(8,128)(2,1)S(1)} %get-tuple-element.134), channel_id=1, source_target_pairs={{32,64},{33,65},{34,66},{35,67},{36,68},{37,69},{38,70},{39,71},{4... | collective-permute-start | bytes 589832 | tf_op jit(solution)/shard_map/ppermute | solution.py:180
  15.0 5.3 %collective-permute-start.7 = (bf16[128,128]{1,0:T(8,128)(2,1)S(1)}, bf16[128,128]{1,0:T(8,128)(2,1)S(1)}, u32[]{:S(2)}, u32[]{:S(2)}) collective-permute-start(bf16[128,128]{1,0:T(8,128)(2,1)S(1)} %get-tuple-element.135), channel_id=1, source_target_pairs={{33,66},{34,65},{35,68},{36,67},{37,70},{38,69},{39,72},{40,71},{4... | collective-permute-start | bytes 98312 | tf_op jit(solution)/shard_map/ppermute | solution.py:181
  15.6 4.7 %collective-permute-start.8 = (bf16[128,128]{1,0:T(8,128)(2,1)S(1)}, bf16[128,128]{1,0:T(8,128)(2,1)S(1)}, u32[]{:S(2)}, u32[]{:S(2)}) collective-permute-start(bf16[128,128]{1,0:T(8,128)(2,1)S(1)} %get-tuple-element.136), channel_id=1, source_target_pairs={{32,65},{33,64},{34,67},{35,66},{36,69},{37,68},{38,71},{39,70},{4... | collective-permute-start | bytes 98312 | tf_op jit(solution)/shard_map/ppermute | solution.py:182
  16.4 18.1 %collective-permute-start.15 = (bf16[128,768]{1,0:T(8,128)(2,1)S(1)}, bf16[128,768]{1,0:T(8,128)(2,1)S(1)}, u32[]{:S(2)}, u32[]{:S(2)}) collective-permute-start(bf16[128,768]{1,0:T(8,128)(2,1)S(1)} %get-tuple-element.145), channel_id=1, source_target_pairs={{64,96},{65,97},{66,98},{67,99},{68,100},{69,101},{70,102},{71,103... | collective-permute-start | bytes 589832 | tf_op jit(solution)/shard_map/ppermute | solution.py:180
  17.7 18.1 %collective-permute-start.16 = (bf16[128,128]{1,0:T(8,128)(2,1)S(1)}, bf16[128,128]{1,0:T(8,128)(2,1)S(1)}, u32[]{:S(2)}, u32[]{:S(2)}) collective-permute-start(bf16[128,128]{1,0:T(8,128)(2,1)S(1)} %get-tuple-element.146), channel_id=1, source_target_pairs={{65,98},{66,97},{67,100},{68,99},{69,102},{70,101},{71,104},{72,10... | collective-permute-start | bytes 98312 | tf_op jit(solution)/shard_map/ppermute | solution.py:181
  19.0 16.8 %collective-permute-start.17 = (bf16[128,128]{1,0:T(8,128)(2,1)S(1)}, bf16[128,128]{1,0:T(8,128)(2,1)S(1)}, u32[]{:S(2)}, u32[]{:S(2)}) collective-permute-start(bf16[128,128]{1,0:T(8,128)(2,1)S(1)} %get-tuple-element.147), channel_id=1, source_target_pairs={{64,97},{65,96},{66,99},{67,98},{68,101},{69,100},{70,103},{71,102... | collective-permute-start | bytes 98312 | tf_op jit(solution)/shard_map/ppermute | solution.py:182
  20.3 20.6 %collective-permute-start.12 = (bf16[128,768]{1,0:T(8,128)(2,1)S(1)}, bf16[128,768]{1,0:T(8,128)(2,1)S(1)}, u32[]{:S(2)}, u32[]{:S(2)}) collective-permute-start(bf16[128,768]{1,0:T(8,128)(2,1)S(1)} %get-tuple-element.142), channel_id=1, source_target_pairs={{64,96},{65,97},{66,98},{67,99},{68,100},{69,101},{70,102},{71,103... | collective-permute-start | bytes 589832 | tf_op jit(solution)/shard_map/ppermute | solution.py:180
  21.6 21.0 %collective-permute-start.13 = (bf16[128,128]{1,0:T(8,128)(2,1)S(1)}, bf16[128,128]{1,0:T(8,128)(2,1)S(1)}, u32[]{:S(2)}, u32[]{:S(2)}) collective-permute-start(bf16[128,128]{1,0:T(8,128)(2,1)S(1)} %get-tuple-element.143), channel_id=1, source_target_pairs={{65,98},{66,97},{67,100},{68,99},{69,102},{70,101},{71,104},{72,10... | collective-permute-start | bytes 98312 | tf_op jit(solution)/shard_map/ppermute | solution.py:181
  34.5 8.2 %collective-permute-start.14 = (bf16[128,128]{1,0:T(8,128)(2,1)S(1)}, bf16[128,128]{1,0:T(8,128)(2,1)S(1)}, u32[]{:S(2)}, u32[]{:S(2)}) collective-permute-start(bf16[128,128]{1,0:T(8,128)(2,1)S(1)} %get-tuple-element.144), channel_id=1, source_target_pairs={{64,97},{65,96},{66,99},{67,98},{68,101},{69,100},{70,103},{71,102... | collective-permute-start | bytes 98312 | tf_op jit(solution)/shard_map/ppermute | solution.py:182
  35.9 8.2 %collective-permute-start.21 = (bf16[128,768]{1,0:T(8,128)(2,1)S(1)}, bf16[128,768]{1,0:T(8,128)(2,1)S(1)}, u32[]{:S(2)}, u32[]{:S(2)}) collective-permute-start(bf16[128,768]{1,0:T(8,128)(2,1)S(1)} %get-tuple-element.153), channel_id=1, source_target_pairs={{96,128},{97,129},{98,130},{99,131},{100,132},{101,133},{102,134},... | collective-permute-start | bytes 589832 | tf_op jit(solution)/shard_map/ppermute | solution.py:180
  36.5 8.2 %collective-permute-start.22 = (bf16[128,128]{1,0:T(8,128)(2,1)S(1)}, bf16[128,128]{1,0:T(8,128)(2,1)S(1)}, u32[]{:S(2)}, u32[]{:S(2)}) collective-permute-start(bf16[128,128]{1,0:T(8,128)(2,1)S(1)} %get-tuple-element.154), channel_id=1, source_target_pairs={{97,130},{98,129},{99,132},{100,131},{101,134},{102,133},{103,136}... | collective-permute-start | bytes 98312 | tf_op jit(solution)/shard_map/ppermute | solution.py:181
  41.0 3.8 %collective-permute-start.23 = (bf16[128,128]{1,0:T(8,128)(2,1)S(1)}, bf16[128,128]{1,0:T(8,128)(2,1)S(1)}, u32[]{:S(2)}, u32[]{:S(2)}) collective-permute-start(bf16[128,128]{1,0:T(8,128)(2,1)S(1)} %get-tuple-element.155), channel_id=1, source_target_pairs={{96,129},{97,128},{98,131},{99,130},{100,133},{101,132},{102,135},... | collective-permute-start | bytes 98312 | tf_op jit(solution)/shard_map/ppermute | solution.py:182
  43.4 3.5 %collective-permute-start.19 = (bf16[128,128]{1,0:T(8,128)(2,1)S(1)}, bf16[128,128]{1,0:T(8,128)(2,1)S(1)}, u32[]{:S(2)}, u32[]{:S(2)}) collective-permute-start(bf16[128,128]{1,0:T(8,128)(2,1)S(1)} %get-tuple-element.151), channel_id=1, source_target_pairs={{97,130},{98,129},{99,132},{100,131},{101,134},{102,133},{103,136}... | collective-permute-start | bytes 98312 | tf_op jit(solution)/shard_map/ppermute | solution.py:181
  45.4 3.5 %collective-permute-start.28 = (bf16[128,128]{1,0:T(8,128)(2,1)S(1)}, bf16[128,128]{1,0:T(8,128)(2,1)S(1)}, u32[]{:S(2)}, u32[]{:S(2)}) collective-permute-start(bf16[128,128]{1,0:T(8,128)(2,1)S(1)} %get-tuple-element.162), channel_id=1, source_target_pairs={{129,162},{130,161},{131,164},{132,163},{133,166},{134,165},{135,1... | collective-permute-start | bytes 98312 | tf_op jit(solution)/shard_map/ppermute | solution.py:181
  47.5 3.5 %collective-permute-start.25 = (bf16[128,128]{1,0:T(8,128)(2,1)S(1)}, bf16[128,128]{1,0:T(8,128)(2,1)S(1)}, u32[]{:S(2)}, u32[]{:S(2)}) collective-permute-start(bf16[128,128]{1,0:T(8,128)(2,1)S(1)} %get-tuple-element.159), channel_id=1, source_target_pairs={{129,162},{130,161},{131,164},{132,163},{133,166},{134,165},{135,1... | collective-permute-start | bytes 98312 | tf_op jit(solution)/shard_map/ppermute | solution.py:181
  49.6 3.5 %collective-permute-start.34 = (bf16[128,128]{1,0:T(8,128)(2,1)S(1)}, bf16[128,128]{1,0:T(8,128)(2,1)S(1)}, u32[]{:S(2)}, u32[]{:S(2)}) collective-permute-start(bf16[128,128]{1,0:T(8,128)(2,1)S(1)} %get-tuple-element.170), channel_id=1, source_target_pairs={{161,194},{162,193},{163,196},{164,195},{165,198},{166,197},{167,2... | collective-permute-start | bytes 98312 | tf_op jit(solution)/shard_map/ppermute | solution.py:181
  51.7 3.5 %collective-permute-start.31 = (bf16[128,128]{1,0:T(8,128)(2,1)S(1)}, bf16[128,128]{1,0:T(8,128)(2,1)S(1)}, u32[]{:S(2)}, u32[]{:S(2)}) collective-permute-start(bf16[128,128]{1,0:T(8,128)(2,1)S(1)} %get-tuple-element.167), channel_id=1, source_target_pairs={{161,194},{162,193},{163,196},{164,195},{165,198},{166,197},{167,2... | collective-permute-start | bytes 98312 | tf_op jit(solution)/shard_map/ppermute | solution.py:181
  53.8 3.5 %collective-permute-start.40 = (bf16[128,128]{1,0:T(8,128)(2,1)S(1)}, bf16[128,128]{1,0:T(8,128)(2,1)S(1)}, u32[]{:S(2)}, u32[]{:S(2)}) collective-permute-start(bf16[128,128]{1,0:T(8,128)(2,1)S(1)} %get-tuple-element.178), channel_id=1, source_target_pairs={{1,34},{2,33},{3,36},{4,35},{5,38},{6,37},{7,40},{8,39},{9,42},{10... | collective-permute-start | bytes 98312 | tf_op jit(solution)/shard_map/ppermute | solution.py:181
  55.9 3.5 %collective-permute-start.37 = (bf16[128,128]{1,0:T(8,128)(2,1)S(1)}, bf16[128,128]{1,0:T(8,128)(2,1)S(1)}, u32[]{:S(2)}, u32[]{:S(2)}) collective-permute-start(bf16[128,128]{1,0:T(8,128)(2,1)S(1)} %get-tuple-element.175), channel_id=1, source_target_pairs={{1,34},{2,33},{3,36},{4,35},{5,38},{6,37},{7,40},{8,39},{9,42},{10... | collective-permute-start | bytes 98312 | tf_op jit(solution)/shard_map/ppermute | solution.py:181
  58.0 3.5 %collective-permute-start.46 = (bf16[128,128]{1,0:T(8,128)(2,1)S(1)}, bf16[128,128]{1,0:T(8,128)(2,1)S(1)}, u32[]{:S(2)}, u32[]{:S(2)}) collective-permute-start(bf16[128,128]{1,0:T(8,128)(2,1)S(1)} %get-tuple-element.186), channel_id=1, source_target_pairs={{33,66},{34,65},{35,68},{36,67},{37,70},{38,69},{39,72},{40,71},{4... | collective-permute-start | bytes 98312 | tf_op jit(solution)/shard_map/ppermute | solution.py:181
  59.4 4.7 %collective-permute-start.42 = (bf16[128,768]{1,0:T(8,128)(2,1)S(1)}, bf16[128,768]{1,0:T(8,128)(2,1)S(1)}, u32[]{:S(2)}, u32[]{:S(2)}) collective-permute-start(bf16[128,768]{1,0:T(8,128)(2,1)S(1)} %get-tuple-element.182), channel_id=1, source_target_pairs={{32,64},{33,65},{34,66},{35,67},{36,68},{37,69},{38,70},{39,71},{4... | collective-permute-start | bytes 589832 | tf_op jit(solution)/shard_map/ppermute | solution.py:180
  60.1 5.3 %collective-permute-start.43 = (bf16[128,128]{1,0:T(8,128)(2,1)S(1)}, bf16[128,128]{1,0:T(8,128)(2,1)S(1)}, u32[]{:S(2)}, u32[]{:S(2)}) collective-permute-start(bf16[128,128]{1,0:T(8,128)(2,1)S(1)} %get-tuple-element.183), channel_id=1, source_target_pairs={{33,66},{34,65},{35,68},{36,67},{37,70},{38,69},{39,72},{40,71},{4... | collective-permute-start | bytes 98312 | tf_op jit(solution)/shard_map/ppermute | solution.py:181
  60.8 4.7 %collective-permute-start.44 = (bf16[128,128]{1,0:T(8,128)(2,1)S(1)}, bf16[128,128]{1,0:T(8,128)(2,1)S(1)}, u32[]{:S(2)}, u32[]{:S(2)}) collective-permute-start(bf16[128,128]{1,0:T(8,128)(2,1)S(1)} %get-tuple-element.184), channel_id=1, source_target_pairs={{32,65},{33,64},{34,67},{35,66},{36,69},{37,68},{38,71},{39,70},{4... | collective-permute-start | bytes 98312 | tf_op jit(solution)/shard_map/ppermute | solution.py:182
  61.5 28.5 %collective-permute-start.51 = (bf16[128,768]{1,0:T(8,128)(2,1)S(1)}, bf16[128,768]{1,0:T(8,128)(2,1)S(1)}, u32[]{:S(2)}, u32[]{:S(2)}) collective-permute-start(bf16[128,768]{1,0:T(8,128)(2,1)S(1)} %get-tuple-element.193), channel_id=1, source_target_pairs={{64,96},{65,97},{66,98},{67,99},{68,100},{69,101},{70,102},{71,103... | collective-permute-start | bytes 589832 | tf_op jit(solution)/shard_map/ppermute | solution.py:180
  62.8 28.8 %collective-permute-start.52 = (bf16[128,128]{1,0:T(8,128)(2,1)S(1)}, bf16[128,128]{1,0:T(8,128)(2,1)S(1)}, u32[]{:S(2)}, u32[]{:S(2)}) collective-permute-start(bf16[128,128]{1,0:T(8,128)(2,1)S(1)} %get-tuple-element.194), channel_id=1, source_target_pairs={{65,98},{66,97},{67,100},{68,99},{69,102},{70,101},{71,104},{72,10... | collective-permute-start | bytes 98312 | tf_op jit(solution)/shard_map/ppermute | solution.py:181
  64.1 27.5 %collective-permute-start.53 = (bf16[128,128]{1,0:T(8,128)(2,1)S(1)}, bf16[128,128]{1,0:T(8,128)(2,1)S(1)}, u32[]{:S(2)}, u32[]{:S(2)}) collective-permute-start(bf16[128,128]{1,0:T(8,128)(2,1)S(1)} %get-tuple-element.195), channel_id=1, source_target_pairs={{64,97},{65,96},{66,99},{67,98},{68,101},{69,100},{70,103},{71,102... | collective-permute-start | bytes 98312 | tf_op jit(solution)/shard_map/ppermute | solution.py:182
  65.5 30.4 %collective-permute-start.48 = (bf16[128,768]{1,0:T(8,128)(2,1)S(1)}, bf16[128,768]{1,0:T(8,128)(2,1)S(1)}, u32[]{:S(2)}, u32[]{:S(2)}) collective-permute-start(bf16[128,768]{1,0:T(8,128)(2,1)S(1)} %get-tuple-element.190), channel_id=1, source_target_pairs={{64,96},{65,97},{66,98},{67,99},{68,100},{69,101},{70,102},{71,103... | collective-permute-start | bytes 589832 | tf_op jit(solution)/shard_map/ppermute | solution.py:180
  66.8 30.3 %collective-permute-start.49 = (bf16[128,128]{1,0:T(8,128)(2,1)S(1)}, bf16[128,128]{1,0:T(8,128)(2,1)S(1)}, u32[]{:S(2)}, u32[]{:S(2)}) collective-permute-start(bf16[128,128]{1,0:T(8,128)(2,1)S(1)} %get-tuple-element.191), channel_id=1, source_target_pairs={{65,98},{66,97},{67,100},{68,99},{69,102},{70,101},{71,104},{72,10... | collective-permute-start | bytes 98312 | tf_op jit(solution)/shard_map/ppermute | solution.py:181
  90.0 7.1 %collective-permute-start.50 = (bf16[128,128]{1,0:T(8,128)(2,1)S(1)}, bf16[128,128]{1,0:T(8,128)(2,1)S(1)}, u32[]{:S(2)}, u32[]{:S(2)}) collective-permute-start(bf16[128,128]{1,0:T(8,128)(2,1)S(1)} %get-tuple-element.192), channel_id=1, source_target_pairs={{64,97},{65,96},{66,99},{67,98},{68,101},{69,100},{70,103},{71,102... | collective-permute-start | bytes 98312 | tf_op jit(solution)/shard_map/ppermute | solution.py:182
  91.6 6.8 %collective-permute-start.57 = (bf16[128,768]{1,0:T(8,128)(2,1)S(1)}, bf16[128,768]{1,0:T(8,128)(2,1)S(1)}, u32[]{:S(2)}, u32[]{:S(2)}) collective-permute-start(bf16[128,768]{1,0:T(8,128)(2,1)S(1)} %get-tuple-element.201), channel_id=1, source_target_pairs={{96,128},{97,129},{98,130},{99,131},{100,132},{101,133},{102,134},... | collective-permute-start | bytes 589832 | tf_op jit(solution)/shard_map/ppermute | solution.py:180
  92.2 6.8 %collective-permute-start.58 = (bf16[128,128]{1,0:T(8,128)(2,1)S(1)}, bf16[128,128]{1,0:T(8,128)(2,1)S(1)}, u32[]{:S(2)}, u32[]{:S(2)}) collective-permute-start(bf16[128,128]{1,0:T(8,128)(2,1)S(1)} %get-tuple-element.202), channel_id=1, source_target_pairs={{97,130},{98,129},{99,132},{100,131},{101,134},{102,133},{103,136}... | collective-permute-start | bytes 98312 | tf_op jit(solution)/shard_map/ppermute | solution.py:181
  97.7 3.5 %collective-permute-start.55 = (bf16[128,128]{1,0:T(8,128)(2,1)S(1)}, bf16[128,128]{1,0:T(8,128)(2,1)S(1)}, u32[]{:S(2)}, u32[]{:S(2)}) collective-permute-start(bf16[128,128]{1,0:T(8,128)(2,1)S(1)} %get-tuple-element.199), channel_id=1, source_target_pairs={{97,130},{98,129},{99,132},{100,131},{101,134},{102,133},{103,136}... | collective-permute-start | bytes 98312 | tf_op jit(solution)/shard_map/ppermute | solution.py:181
  99.8 3.5 %collective-permute-start.64 = (bf16[128,128]{1,0:T(8,128)(2,1)S(1)}, bf16[128,128]{1,0:T(8,128)(2,1)S(1)}, u32[]{:S(2)}, u32[]{:S(2)}) collective-permute-start(bf16[128,128]{1,0:T(8,128)(2,1)S(1)} %get-tuple-element.210), channel_id=1, source_target_pairs={{129,162},{130,161},{131,164},{132,163},{133,166},{134,165},{135,1... | collective-permute-start | bytes 98312 | tf_op jit(solution)/shard_map/ppermute | solution.py:181
  101.9 3.5 %collective-permute-start.61 = (bf16[128,128]{1,0:T(8,128)(2,1)S(1)}, bf16[128,128]{1,0:T(8,128)(2,1)S(1)}, u32[]{:S(2)}, u32[]{:S(2)}) collective-permute-start(bf16[128,128]{1,0:T(8,128)(2,1)S(1)} %get-tuple-element.207), channel_id=1, source_target_pairs={{129,162},{130,161},{131,164},{132,163},{133,166},{134,165},{135,1... | collective-permute-start | bytes 98312 | tf_op jit(solution)/shard_map/ppermute | solution.py:181
  113.8 4.7 %collective-permute-start.78 = (bf16[128,768]{1,0:T(8,128)(2,1)S(1)}, bf16[128,768]{1,0:T(8,128)(2,1)S(1)}, u32[]{:S(2)}, u32[]{:S(2)}) collective-permute-start(bf16[128,768]{1,0:T(8,128)(2,1)S(1)} %get-tuple-element.230), channel_id=1, source_target_pairs={{32,64},{33,65},{34,66},{35,67},{36,68},{37,69},{38,70},{39,71},{4... | collective-permute-start | bytes 589832 | tf_op jit(solution)/shard_map/ppermute | solution.py:180
  114.4 5.3 %collective-permute-start.79 = (bf16[128,128]{1,0:T(8,128)(2,1)S(1)}, bf16[128,128]{1,0:T(8,128)(2,1)S(1)}, u32[]{:S(2)}, u32[]{:S(2)}) collective-permute-start(bf16[128,128]{1,0:T(8,128)(2,1)S(1)} %get-tuple-element.231), channel_id=1, source_target_pairs={{33,66},{34,65},{35,68},{36,67},{37,70},{38,69},{39,72},{40,71},{4... | collective-permute-start | bytes 98312 | tf_op jit(solution)/shard_map/ppermute | solution.py:181
  115.1 4.7 %collective-permute-start.80 = (bf16[128,128]{1,0:T(8,128)(2,1)S(1)}, bf16[128,128]{1,0:T(8,128)(2,1)S(1)}, u32[]{:S(2)}, u32[]{:S(2)}) collective-permute-start(bf16[128,128]{1,0:T(8,128)(2,1)S(1)} %get-tuple-element.232), channel_id=1, source_target_pairs={{32,65},{33,64},{34,67},{35,66},{36,69},{37,68},{38,71},{39,70},{4... | collective-permute-start | bytes 98312 | tf_op jit(solution)/shard_map/ppermute | solution.py:182
  115.9 31.1 %collective-permute-start.88 = (bf16[128,128]{1,0:T(8,128)(2,1)S(1)}, bf16[128,128]{1,0:T(8,128)(2,1)S(1)}, u32[]{:S(2)}, u32[]{:S(2)}) collective-permute-start(bf16[128,128]{1,0:T(8,128)(2,1)S(1)} %get-tuple-element.242), channel_id=1, source_target_pairs={{65,98},{66,97},{67,100},{68,99},{69,102},{70,101},{71,104},{72,10... | collective-permute-start | bytes 98312 | tf_op jit(solution)/shard_map/ppermute | solution.py:181
  117.2 28.5 %collective-permute-start.87 = (bf16[128,768]{1,0:T(8,128)(2,1)S(1)}, bf16[128,768]{1,0:T(8,128)(2,1)S(1)}, u32[]{:S(2)}, u32[]{:S(2)}) collective-permute-start(bf16[128,768]{1,0:T(8,128)(2,1)S(1)} %get-tuple-element.241), channel_id=1, source_target_pairs={{64,96},{65,97},{66,98},{67,99},{68,100},{69,101},{70,102},{71,103... | collective-permute-start | bytes 589832 | tf_op jit(solution)/shard_map/ppermute | solution.py:180
  118.5 28.5 %collective-permute-start.89 = (bf16[128,128]{1,0:T(8,128)(2,1)S(1)}, bf16[128,128]{1,0:T(8,128)(2,1)S(1)}, u32[]{:S(2)}, u32[]{:S(2)}) collective-permute-start(bf16[128,128]{1,0:T(8,128)(2,1)S(1)} %get-tuple-element.243), channel_id=1, source_target_pairs={{64,97},{65,96},{66,99},{67,98},{68,101},{69,100},{70,103},{71,102... | collective-permute-start | bytes 98312 | tf_op jit(solution)/shard_map/ppermute | solution.py:182
  119.8 30.1 %collective-permute-start.84 = (bf16[128,768]{1,0:T(8,128)(2,1)S(1)}, bf16[128,768]{1,0:T(8,128)(2,1)S(1)}, u32[]{:S(2)}, u32[]{:S(2)}) collective-permute-start(bf16[128,768]{1,0:T(8,128)(2,1)S(1)} %get-tuple-element.238), channel_id=1, source_target_pairs={{64,96},{65,97},{66,98},{67,99},{68,100},{69,101},{70,102},{71,103... | collective-permute-start | bytes 589832 | tf_op jit(solution)/shard_map/ppermute | solution.py:180
  121.1 30.6 %collective-permute-start.85 = (bf16[128,128]{1,0:T(8,128)(2,1)S(1)}, bf16[128,128]{1,0:T(8,128)(2,1)S(1)}, u32[]{:S(2)}, u32[]{:S(2)}) collective-permute-start(bf16[128,128]{1,0:T(8,128)(2,1)S(1)} %get-tuple-element.239), channel_id=1, source_target_pairs={{65,98},{66,97},{67,100},{68,99},{69,102},{70,101},{71,104},{72,10... | collective-permute-start | bytes 98312 | tf_op jit(solution)/shard_map/ppermute | solution.py:181
  145.6 6.1 %collective-permute-start.86 = (bf16[128,128]{1,0:T(8,128)(2,1)S(1)}, bf16[128,128]{1,0:T(8,128)(2,1)S(1)}, u32[]{:S(2)}, u32[]{:S(2)}) collective-permute-start(bf16[128,128]{1,0:T(8,128)(2,1)S(1)} %get-tuple-element.240), channel_id=1, source_target_pairs={{64,97},{65,96},{66,99},{67,98},{68,101},{69,100},{70,103},{71,102... | collective-permute-start | bytes 98312 | tf_op jit(solution)/shard_map/ppermute | solution.py:182
  (42 other events, 132.6 us)

commit v2 on v1

--- a/solution.py
+++ b/solution.py
@@ -20,12 +20,11 @@
     return lax.dot_general(x, y, NT, preferred_element_type=jnp.float32)
 
 
-def load(pairs, sems):
+def loads(pairs, sems):
     copies = [pltpu.make_async_copy(src, dst, sems.at[i]) for i, (src, dst) in enumerate(pairs)]
     for copy in copies:
         copy.start()
-    for copy in copies:
-        copy.wait()
+    return copies
 
 
 def substitute(out, known, sup, inv, a):
@@ -37,15 +36,25 @@
 
 
 def sides_kernel(rhs_hbm, inv_hbm, sup_hbm, gt, rhs, inv, sup, sems):
-    load(((inv_hbm, inv), (rhs_hbm, rhs), (sup_hbm, sup)), sems)
+    *early, late = loads(((inv_hbm, inv), (rhs_hbm, rhs), (sup_hbm, sup)), sems)
+    for copy in early:
+        copy.wait()
     for a in range(BD):
+        if a == 1:
+            late.wait()
         substitute(gt, rhs[a].T.astype(jnp.float32), sup, inv, a)
 
 
 def matrix_kernel(pattern_hbm, inv_hbm, cpl_hbm, sup_hbm, ht, ct, pattern, inv, cpl, sup, sems):
-    load(((pattern_hbm, pattern), (inv_hbm, inv), (sup_hbm, sup), (cpl_hbm, cpl)), sems)
+    rows = [(cpl_hbm.at[a], cpl.at[a]) for a in range(BD)]
+    *early, late = loads(((pattern_hbm, pattern), (inv_hbm, inv), *rows, (sup_hbm, sup)), sems)
+    for copy in early[:2]:
+        copy.wait()
     first = lax.axis_index("row") * BD - 1
     for a in range(BD):
+        early[2 + a].wait()
+        if a == 1:
+            late.wait()
         ct[...] = jnp.zeros_like(ct)
 
         @pl.when(lax.axis_index("sec") > 0)
@@ -62,7 +71,10 @@
 
 
 def step_kernel(tick, rows, last, matrix, *refs):
-    if last:
+    out = None
+    if last == "whole":
+        *arrived, ht, _, out, gt = refs
+    elif last:
         *arrived, ht, _, gt = refs
     else:
         *arrived, ht, _, own, cross, mate, gt = refs if matrix else (*refs[:1], *refs)
@@ -89,10 +101,9 @@
             if not last:
                 emit(value)
 
-
-def finish_kernel(gt, out):
-    for a in range(BD):
-        out[a] = gt[:, a * BLK : (a + 1) * BLK].T
+    if out is not None:
+        for a in range(BD):
+            out[a] = gt[:, a * BLK : (a + 1) * BLK].T
 
 
 def local(right_sides, inverses, coupling, supernode_blocks, pattern):
@@ -116,7 +127,7 @@
             out_specs=vmem,
             scratch_shapes=scratch
             + [(pltpu.SMEM if x is pattern else pltpu.VMEM)(x.shape, x.dtype) for x in operands]
-            + [pltpu.SemaphoreType.DMA((len(operands),))],
+            + [pltpu.SemaphoreType.DMA((BD + 3,))],
             compiler_params=params,
             cost_estimate=pl.CostEstimate(flops=flops, bytes_accessed=2**21, transcendentals=0),
             name=name,
@@ -147,8 +158,8 @@
     def step(tick, start, wide, arrived, gt):
         matrix = bool(arrived) or start > 0
         operands = (*arrived, ht, gt) if matrix else (gt,)
-        last = tick == sections - 1
-        results = [] if last else [pltpu.VMEM((wide, columns), bf16) for columns in (BD * BLK, BLK, BLK)]
+        last = "" if tick < sections - 1 else "whole" if start + wide == nrhs else "chunk"
+        results = [jax.ShapeDtypeStruct((BD, BLK, nrhs), bf16)] * (last == "whole") if last else [pltpu.VMEM((wide, columns), bf16) for columns in (BD * BLK, BLK, BLK)]
         results.append(pltpu.VMEM((nrhs, BD * BLK), bf16))
         return pl.pallas_call(
             functools.partial(step_kernel, tick, slice(start, start + wide), last, matrix),
@@ -174,21 +185,14 @@
     for tick in range(sections):
         for k, (start, wide) in enumerate(zip(starts, CHUNKS)):
             *outgoing, gt = step(tick, start, wide, arrived[k], gt)
-            if outgoing:
+            if tick < sections - 1:
                 own, cross, mate = outgoing
                 arrived[k] = (
                     settled(lax.ppermute(own, ("sec", "row"), route(tick, lambda d: d))),
                     lax.ppermute(cross, ("sec", "row"), route(tick, lambda d: d + 1 if d % 2 else d - 1)),
                     lax.ppermute(mate, ("sec", "row"), route(tick, lambda d: d ^ 1)),
                 )
-    return pl.pallas_call(
-        finish_kernel,
-        out_shape=jax.ShapeDtypeStruct((BD, BLK, nrhs), bf16),
-        in_specs=[vmem],
-        out_specs=vmem,
-        compiler_params=params,
-        name="finish",
-    )(gt)
+    return outgoing[0]
 
 
 def solution(mesh):

time: 154 us -> 154 us (level)
  no operation moved by 1% of the time
where the time goes in v2:
time: 154 us; the launch traced here: 153 us
  starting transfers between devices  71.3 us (46%)
  waiting for transfers between devices  69.5 us (45%)
  Pallas kernels  10.2 us (7%)
  between operations  1.79 us (1%)
    ppermute x30, waiting for transfers between devices, local(): lax.ppermute(own, ('sec', 'row'), route(tick, lambda d: d))  65.7 us
    ppermute x30, starting transfers between devices, local(): lax.ppermute(own, ('sec', 'row'), route(tick, lambda d: d))  24.1 us
    ppermute x30, starting transfers between devices, local(): lax.ppermute(cross, ('sec', 'row'), route(tick, lambda d: d + 1 if d % 2...  23.7 us
    ppermute x30, starting transfers between devices, local(): lax.ppermute(mate, ('sec', 'row'), route(tick, lambda d: d ^ 1))  23.6 us
    pallas_call x2, Pallas kernels, prepared(): pl.pallas_call(kernel, out_shape=pltpu.VMEM((rows, BD * BLK), bf16), in_s...  7.94 us
    ppermute x30, waiting for transfers between devices, local(): lax.ppermute(cross, ('sec', 'row'), route(tick, lambda d: d + 1 if d % 2...  3.73 us
  transfers between devices with their start and end apart: 90, of which 10 were waited for; matrix products, arithmetic and copies ran while one was open for 0% of the time, Pallas kernels for 4%

profile of v2, /device:TPU:482, one launch (start us, length us, event | category | flops | bytes accessed | tf_op | source)
XLA Modules:
  0.0 152.8 jit_solution(3312168900581706116)
XLA Ops:
  0.0 2.7 %sides.1.refs_0_ = bf16[256,768]{1,0:T(8,128)(2,1)S(1)} custom-call(bf16[6,128,256]{2,1,0:T(8,128)(2,1)} %rhs_hbm.1, bf16[6,128,128]{2,1,0:T(8,128)(2,1)} %inv_hbm.3, bf16[15,128,128]{2,1,0:T(8,128)(2,1)} %sup_hbm.3), custom_call_target="tpu_custom_call" | custom-call | flops 268435456 | bytes 2097152 | tf_op jit(solution)/shard_map/sides/pallas_call | solution.py:123
  4.1 0.7 collective-permute-start.3
  4.8 5.2 %matrix.1.refs_0_.refs_3_ = bf16[1024,768]{1,0:T(8,128)(2,1)S(1)} custom-call(s32[6,5]{1,0:T(8,128)} %pattern_hbm.1, bf16[6,128,128]{2,1,0:T(8,128)(2,1)} %inv_hbm.3, bf16[6,5,128,128]{3,2,1,0:T(8,128)(2,1)} %cpl_hbm.1, bf16[15,128,128]{2,1,0:T(8,128)(2,1)} %sup_hbm.3), custom_call_target="tpu_custom_call" | custom-call | flops 1900000000 | bytes 2097152 | tf_op jit(solution)/shard_map/matrix/pallas_call | solution.py:123
  10.0 0.7 collective-permute-start
  12.1 0.7 collective-permute-start.9
  14.2 0.7 collective-permute-start.6
  16.3 1.3 collective-permute-start.15
  17.6 1.3 collective-permute-start.16
  18.9 1.3 collective-permute-start.17
  20.3 1.3 collective-permute-start.12
  21.6 1.3 collective-permute-start.13
  22.9 11.6 %collective-permute-done.15._ = bf16[128,768]{1,0:T(8,128)(2,1)S(1)} collective-permute-done((bf16[128,768]{1,0:T(8,128)(2,1)S(1)}, bf16[128,768]{1,0:T(8,128)(2,1)S(1)}, u32[]{:S(2)}, u32[]{:S(2)}) %collective-permute-start.15) | collective-permute-done | bytes 196640 | tf_op jit(solution)/shard_map/ppermute | solution.py:191
  34.5 1.3 collective-permute-start.14
  35.8 0.7 collective-permute-start.21
  37.2 3.7 %collective-permute-done.12._ = bf16[128,768]{1,0:T(8,128)(2,1)S(1)} collective-permute-done((bf16[128,768]{1,0:T(8,128)(2,1)S(1)}, bf16[128,768]{1,0:T(8,128)(2,1)S(1)}, u32[]{:S(2)}, u32[]{:S(2)}) %collective-permute-start.12) | collective-permute-done | bytes 196640 | tf_op jit(solution)/shard_map/ppermute | solution.py:191
  41.6 1.1 collective-permute-done.13.refs_1_
  44.7 0.7 collective-permute-start.27
  46.8 0.7 collective-permute-start.24
  48.9 0.7 collective-permute-start.33
  51.0 0.7 collective-permute-start.30
  53.1 0.7 collective-permute-start.39
  55.2 0.7 collective-permute-start.36
  57.3 0.7 collective-permute-start.45
  59.3 0.7 collective-permute-start.42
  61.4 1.3 collective-permute-start.51
  62.7 1.3 collective-permute-start.52
  64.0 1.3 collective-permute-start.53
  65.4 1.5 collective-permute-start.48
  66.9 1.3 collective-permute-start.49
  68.2 21.7 %collective-permute-done.51._ = bf16[128,768]{1,0:T(8,128)(2,1)S(1)} collective-permute-done((bf16[128,768]{1,0:T(8,128)(2,1)S(1)}, bf16[128,768]{1,0:T(8,128)(2,1)S(1)}, u32[]{:S(2)}, u32[]{:S(2)}) %collective-permute-start.51) | collective-permute-done | bytes 196640 | tf_op jit(solution)/shard_map/ppermute | solution.py:191
  89.9 1.3 collective-permute-start.50
  92.9 3.0 %collective-permute-done.48._ = bf16[128,768]{1,0:T(8,128)(2,1)S(1)} collective-permute-done((bf16[128,768]{1,0:T(8,128)(2,1)S(1)}, bf16[128,768]{1,0:T(8,128)(2,1)S(1)}, u32[]{:S(2)}, u32[]{:S(2)}) %collective-permute-start.48) | collective-permute-done | bytes 196640 | tf_op jit(solution)/shard_map/ppermute | solution.py:191
  99.1 0.7 collective-permute-start.63
  101.2 0.7 collective-permute-start.60
  103.3 0.7 collective-permute-start.69
  105.3 0.7 collective-permute-start.66
  107.4 0.7 collective-permute-start.75
  109.5 0.7 collective-permute-start.72
  115.8 1.3 collective-permute-start.88
  117.1 1.3 collective-permute-start.87
  118.4 1.3 collective-permute-start.89
  119.8 1.3 collective-permute-start.84
  121.1 1.3 collective-permute-start.85
  122.4 22.9 %collective-permute-done.87._ = bf16[128,768]{1,0:T(8,128)(2,1)S(1)} collective-permute-done((bf16[128,768]{1,0:T(8,128)(2,1)S(1)}, bf16[128,768]{1,0:T(8,128)(2,1)S(1)}, u32[]{:S(2)}, u32[]{:S(2)}) %collective-permute-start.87) | collective-permute-done | bytes 196640 | tf_op jit(solution)/shard_map/ppermute | solution.py:191
  145.3 1.3 collective-permute-start.86
  147.0 2.7 %collective-permute-done.84._ = bf16[128,768]{1,0:T(8,128)(2,1)S(1)} collective-permute-done((bf16[128,768]{1,0:T(8,128)(2,1)S(1)}, bf16[128,768]{1,0:T(8,128)(2,1)S(1)}, u32[]{:S(2)}, u32[]{:S(2)}) %collective-permute-start.84) | collective-permute-done | bytes 196640 | tf_op jit(solution)/shard_map/ppermute | solution.py:191
  149.7 1.8 %collective-permute-done.85.refs_1_ = bf16[128,128]{1,0:T(8,128)(2,1)S(1)} collective-permute-done((bf16[128,128]{1,0:T(8,128)(2,1)S(1)}, bf16[128,128]{1,0:T(8,128)(2,1)S(1)}, u32[]{:S(2)}, u32[]{:S(2)}) %collective-permute-start.85) | collective-permute-done | bytes 32800 | tf_op jit(solution)/shard_map/ppermute | solution.py:192
  151.5 1.3 step.63
  (196 shorter events, 37.1 us)
Async XLA Ops:
  2.8 9.3 %collective-permute-start.4 = (bf16[128,128]{1,0:T(8,128)(2,1)S(1)}, bf16[128,128]{1,0:T(8,128)(2,1)S(1)}, u32[]{:S(2)}, u32[]{:S(2)}) collective-permute-start(bf16[128,128]{1,0:T(8,128)(2,1)S(1)} %get-tuple-element.131), channel_id=1, source_target_pairs={{1,34},{2,33},{3,36},{4,35},{5,38},{6,37},{7,40},{8,39},{9,42},{10... | collective-permute-start | bytes 98312 | tf_op jit(solution)/shard_map/ppermute | solution.py:192
  3.4 8.7 %collective-permute-start.5 = (bf16[128,128]{1,0:T(8,128)(2,1)S(1)}, bf16[128,128]{1,0:T(8,128)(2,1)S(1)}, u32[]{:S(2)}, u32[]{:S(2)}) collective-permute-start(bf16[128,128]{1,0:T(8,128)(2,1)S(1)} %get-tuple-element.132), channel_id=1, source_target_pairs={{0,33},{1,32},{2,35},{3,34},{4,37},{5,36},{6,39},{7,38},{8,41},{9,... | collective-permute-start | bytes 98312 | tf_op jit(solution)/shard_map/ppermute | solution.py:193
  4.1 7.3 %collective-permute-start.3 = (bf16[128,768]{1,0:T(8,128)(2,1)S(1)}, bf16[128,768]{1,0:T(8,128)(2,1)S(1)}, u32[]{:S(2)}, u32[]{:S(2)}) collective-permute-start(bf16[128,768]{1,0:T(8,128)(2,1)S(1)} %get-tuple-element.130), channel_id=1, source_target_pairs={{0,32},{1,33},{2,34},{3,35},{4,36},{5,37},{6,38},{7,39},{8,40},{9,... | collective-permute-start | bytes 589832 | tf_op jit(solution)/shard_map/ppermute | solution.py:191
  10.7 3.5 %collective-permute-start.1 = (bf16[128,128]{1,0:T(8,128)(2,1)S(1)}, bf16[128,128]{1,0:T(8,128)(2,1)S(1)}, u32[]{:S(2)}, u32[]{:S(2)}) collective-permute-start(bf16[128,128]{1,0:T(8,128)(2,1)S(1)} %get-tuple-element.128), channel_id=1, source_target_pairs={{1,34},{2,33},{3,36},{4,35},{5,38},{6,37},{7,40},{8,39},{9,42},{10... | collective-permute-start | bytes 98312 | tf_op jit(solution)/shard_map/ppermute | solution.py:192
  12.8 3.5 %collective-permute-start.10 = (bf16[128,128]{1,0:T(8,128)(2,1)S(1)}, bf16[128,128]{1,0:T(8,128)(2,1)S(1)}, u32[]{:S(2)}, u32[]{:S(2)}) collective-permute-start(bf16[128,128]{1,0:T(8,128)(2,1)S(1)} %get-tuple-element.139), channel_id=1, source_target_pairs={{33,66},{34,65},{35,68},{36,67},{37,70},{38,69},{39,72},{40,71},{4... | collective-permute-start | bytes 98312 | tf_op jit(solution)/shard_map/ppermute | solution.py:192
  14.2 4.7 %collective-permute-start.6 = (bf16[128,768]{1,0:T(8,128)(2,1)S(1)}, bf16[128,768]{1,0:T(8,128)(2,1)S(1)}, u32[]{:S(2)}, u32[]{:S(2)}) collective-permute-start(bf16[128,768]{1,0:T(8,128)(2,1)S(1)} %get-tuple-element.135), channel_id=1, source_target_pairs={{32,64},{33,65},{34,66},{35,67},{36,68},{37,69},{38,70},{39,71},{4... | collective-permute-start | bytes 589832 | tf_op jit(solution)/shard_map/ppermute | solution.py:191
  14.9 5.3 %collective-permute-start.7 = (bf16[128,128]{1,0:T(8,128)(2,1)S(1)}, bf16[128,128]{1,0:T(8,128)(2,1)S(1)}, u32[]{:S(2)}, u32[]{:S(2)}) collective-permute-start(bf16[128,128]{1,0:T(8,128)(2,1)S(1)} %get-tuple-element.136), channel_id=1, source_target_pairs={{33,66},{34,65},{35,68},{36,67},{37,70},{38,69},{39,72},{40,71},{4... | collective-permute-start | bytes 98312 | tf_op jit(solution)/shard_map/ppermute | solution.py:192
  15.6 4.7 %collective-permute-start.8 = (bf16[128,128]{1,0:T(8,128)(2,1)S(1)}, bf16[128,128]{1,0:T(8,128)(2,1)S(1)}, u32[]{:S(2)}, u32[]{:S(2)}) collective-permute-start(bf16[128,128]{1,0:T(8,128)(2,1)S(1)} %get-tuple-element.137), channel_id=1, source_target_pairs={{32,65},{33,64},{34,67},{35,66},{36,69},{37,68},{38,71},{39,70},{4... | collective-permute-start | bytes 98312 | tf_op jit(solution)/shard_map/ppermute | solution.py:193
  16.3 18.2 %collective-permute-start.15 = (bf16[128,768]{1,0:T(8,128)(2,1)S(1)}, bf16[128,768]{1,0:T(8,128)(2,1)S(1)}, u32[]{:S(2)}, u32[]{:S(2)}) collective-permute-start(bf16[128,768]{1,0:T(8,128)(2,1)S(1)} %get-tuple-element.146), channel_id=1, source_target_pairs={{64,96},{65,97},{66,98},{67,99},{68,100},{69,101},{70,102},{71,103... | collective-permute-start | bytes 589832 | tf_op jit(solution)/shard_map/ppermute | solution.py:191
  17.6 18.2 %collective-permute-start.16 = (bf16[128,128]{1,0:T(8,128)(2,1)S(1)}, bf16[128,128]{1,0:T(8,128)(2,1)S(1)}, u32[]{:S(2)}, u32[]{:S(2)}) collective-permute-start(bf16[128,128]{1,0:T(8,128)(2,1)S(1)} %get-tuple-element.147), channel_id=1, source_target_pairs={{65,98},{66,97},{67,100},{68,99},{69,102},{70,101},{71,104},{72,10... | collective-permute-start | bytes 98312 | tf_op jit(solution)/shard_map/ppermute | solution.py:192
  18.9 16.9 %collective-permute-start.17 = (bf16[128,128]{1,0:T(8,128)(2,1)S(1)}, bf16[128,128]{1,0:T(8,128)(2,1)S(1)}, u32[]{:S(2)}, u32[]{:S(2)}) collective-permute-start(bf16[128,128]{1,0:T(8,128)(2,1)S(1)} %get-tuple-element.148), channel_id=1, source_target_pairs={{64,97},{65,96},{66,99},{67,98},{68,101},{69,100},{70,103},{71,102... | collective-permute-start | bytes 98312 | tf_op jit(solution)/shard_map/ppermute | solution.py:193
  20.3 20.6 %collective-permute-start.12 = (bf16[128,768]{1,0:T(8,128)(2,1)S(1)}, bf16[128,768]{1,0:T(8,128)(2,1)S(1)}, u32[]{:S(2)}, u32[]{:S(2)}) collective-permute-start(bf16[128,768]{1,0:T(8,128)(2,1)S(1)} %get-tuple-element.143), channel_id=1, source_target_pairs={{64,96},{65,97},{66,98},{67,99},{68,100},{69,101},{70,102},{71,103... | collective-permute-start | bytes 589832 | tf_op jit(solution)/shard_map/ppermute | solution.py:191
  21.6 21.0 %collective-permute-start.13 = (bf16[128,128]{1,0:T(8,128)(2,1)S(1)}, bf16[128,128]{1,0:T(8,128)(2,1)S(1)}, u32[]{:S(2)}, u32[]{:S(2)}) collective-permute-start(bf16[128,128]{1,0:T(8,128)(2,1)S(1)} %get-tuple-element.144), channel_id=1, source_target_pairs={{65,98},{66,97},{67,100},{68,99},{69,102},{70,101},{71,104},{72,10... | collective-permute-start | bytes 98312 | tf_op jit(solution)/shard_map/ppermute | solution.py:192
  34.5 8.2 %collective-permute-start.14 = (bf16[128,128]{1,0:T(8,128)(2,1)S(1)}, bf16[128,128]{1,0:T(8,128)(2,1)S(1)}, u32[]{:S(2)}, u32[]{:S(2)}) collective-permute-start(bf16[128,128]{1,0:T(8,128)(2,1)S(1)} %get-tuple-element.145), channel_id=1, source_target_pairs={{64,97},{65,96},{66,99},{67,98},{68,101},{69,100},{70,103},{71,102... | collective-permute-start | bytes 98312 | tf_op jit(solution)/shard_map/ppermute | solution.py:193
  35.8 8.2 %collective-permute-start.21 = (bf16[128,768]{1,0:T(8,128)(2,1)S(1)}, bf16[128,768]{1,0:T(8,128)(2,1)S(1)}, u32[]{:S(2)}, u32[]{:S(2)}) collective-permute-start(bf16[128,768]{1,0:T(8,128)(2,1)S(1)} %get-tuple-element.154), channel_id=1, source_target_pairs={{96,128},{97,129},{98,130},{99,131},{100,132},{101,133},{102,134},... | collective-permute-start | bytes 589832 | tf_op jit(solution)/shard_map/ppermute | solution.py:191
  36.5 8.2 %collective-permute-start.22 = (bf16[128,128]{1,0:T(8,128)(2,1)S(1)}, bf16[128,128]{1,0:T(8,128)(2,1)S(1)}, u32[]{:S(2)}, u32[]{:S(2)}) collective-permute-start(bf16[128,128]{1,0:T(8,128)(2,1)S(1)} %get-tuple-element.155), channel_id=1, source_target_pairs={{97,130},{98,129},{99,132},{100,131},{101,134},{102,133},{103,136}... | collective-permute-start | bytes 98312 | tf_op jit(solution)/shard_map/ppermute | solution.py:192
  40.9 3.8 %collective-permute-start.23 = (bf16[128,128]{1,0:T(8,128)(2,1)S(1)}, bf16[128,128]{1,0:T(8,128)(2,1)S(1)}, u32[]{:S(2)}, u32[]{:S(2)}) collective-permute-start(bf16[128,128]{1,0:T(8,128)(2,1)S(1)} %get-tuple-element.156), channel_id=1, source_target_pairs={{96,129},{97,128},{98,131},{99,130},{100,133},{101,132},{102,135},... | collective-permute-start | bytes 98312 | tf_op jit(solution)/shard_map/ppermute | solution.py:193
  43.3 3.5 %collective-permute-start.19 = (bf16[128,128]{1,0:T(8,128)(2,1)S(1)}, bf16[128,128]{1,0:T(8,128)(2,1)S(1)}, u32[]{:S(2)}, u32[]{:S(2)}) collective-permute-start(bf16[128,128]{1,0:T(8,128)(2,1)S(1)} %get-tuple-element.152), channel_id=1, source_target_pairs={{97,130},{98,129},{99,132},{100,131},{101,134},{102,133},{103,136}... | collective-permute-start | bytes 98312 | tf_op jit(solution)/shard_map/ppermute | solution.py:192
  45.4 3.5 %collective-permute-start.28 = (bf16[128,128]{1,0:T(8,128)(2,1)S(1)}, bf16[128,128]{1,0:T(8,128)(2,1)S(1)}, u32[]{:S(2)}, u32[]{:S(2)}) collective-permute-start(bf16[128,128]{1,0:T(8,128)(2,1)S(1)} %get-tuple-element.163), channel_id=1, source_target_pairs={{129,162},{130,161},{131,164},{132,163},{133,166},{134,165},{135,1... | collective-permute-start | bytes 98312 | tf_op jit(solution)/shard_map/ppermute | solution.py:192
  47.5 3.5 %collective-permute-start.25 = (bf16[128,128]{1,0:T(8,128)(2,1)S(1)}, bf16[128,128]{1,0:T(8,128)(2,1)S(1)}, u32[]{:S(2)}, u32[]{:S(2)}) collective-permute-start(bf16[128,128]{1,0:T(8,128)(2,1)S(1)} %get-tuple-element.160), channel_id=1, source_target_pairs={{129,162},{130,161},{131,164},{132,163},{133,166},{134,165},{135,1... | collective-permute-start | bytes 98312 | tf_op jit(solution)/shard_map/ppermute | solution.py:192
  49.6 3.5 %collective-permute-start.34 = (bf16[128,128]{1,0:T(8,128)(2,1)S(1)}, bf16[128,128]{1,0:T(8,128)(2,1)S(1)}, u32[]{:S(2)}, u32[]{:S(2)}) collective-permute-start(bf16[128,128]{1,0:T(8,128)(2,1)S(1)} %get-tuple-element.171), channel_id=1, source_target_pairs={{161,194},{162,193},{163,196},{164,195},{165,198},{166,197},{167,2... | collective-permute-start | bytes 98312 | tf_op jit(solution)/shard_map/ppermute | solution.py:192
  51.7 3.5 %collective-permute-start.31 = (bf16[128,128]{1,0:T(8,128)(2,1)S(1)}, bf16[128,128]{1,0:T(8,128)(2,1)S(1)}, u32[]{:S(2)}, u32[]{:S(2)}) collective-permute-start(bf16[128,128]{1,0:T(8,128)(2,1)S(1)} %get-tuple-element.168), channel_id=1, source_target_pairs={{161,194},{162,193},{163,196},{164,195},{165,198},{166,197},{167,2... | collective-permute-start | bytes 98312 | tf_op jit(solution)/shard_map/ppermute | solution.py:192
  53.8 3.5 %collective-permute-start.40 = (bf16[128,128]{1,0:T(8,128)(2,1)S(1)}, bf16[128,128]{1,0:T(8,128)(2,1)S(1)}, u32[]{:S(2)}, u32[]{:S(2)}) collective-permute-start(bf16[128,128]{1,0:T(8,128)(2,1)S(1)} %get-tuple-element.179), channel_id=1, source_target_pairs={{1,34},{2,33},{3,36},{4,35},{5,38},{6,37},{7,40},{8,39},{9,42},{10... | collective-permute-start | bytes 98312 | tf_op jit(solution)/shard_map/ppermute | solution.py:192
  55.8 3.5 %collective-permute-start.37 = (bf16[128,128]{1,0:T(8,128)(2,1)S(1)}, bf16[128,128]{1,0:T(8,128)(2,1)S(1)}, u32[]{:S(2)}, u32[]{:S(2)}) collective-permute-start(bf16[128,128]{1,0:T(8,128)(2,1)S(1)} %get-tuple-element.176), channel_id=1, source_target_pairs={{1,34},{2,33},{3,36},{4,35},{5,38},{6,37},{7,40},{8,39},{9,42},{10... | collective-permute-start | bytes 98312 | tf_op jit(solution)/shard_map/ppermute | solution.py:192
  57.9 3.5 %collective-permute-start.46 = (bf16[128,128]{1,0:T(8,128)(2,1)S(1)}, bf16[128,128]{1,0:T(8,128)(2,1)S(1)}, u32[]{:S(2)}, u32[]{:S(2)}) collective-permute-start(bf16[128,128]{1,0:T(8,128)(2,1)S(1)} %get-tuple-element.187), channel_id=1, source_target_pairs={{33,66},{34,65},{35,68},{36,67},{37,70},{38,69},{39,72},{40,71},{4... | collective-permute-start | bytes 98312 | tf_op jit(solution)/shard_map/ppermute | solution.py:192
  59.3 4.7 %collective-permute-start.42 = (bf16[128,768]{1,0:T(8,128)(2,1)S(1)}, bf16[128,768]{1,0:T(8,128)(2,1)S(1)}, u32[]{:S(2)}, u32[]{:S(2)}) collective-permute-start(bf16[128,768]{1,0:T(8,128)(2,1)S(1)} %get-tuple-element.183), channel_id=1, source_target_pairs={{32,64},{33,65},{34,66},{35,67},{36,68},{37,69},{38,70},{39,71},{4... | collective-permute-start | bytes 589832 | tf_op jit(solution)/shard_map/ppermute | solution.py:191
  60.0 5.3 %collective-permute-start.43 = (bf16[128,128]{1,0:T(8,128)(2,1)S(1)}, bf16[128,128]{1,0:T(8,128)(2,1)S(1)}, u32[]{:S(2)}, u32[]{:S(2)}) collective-permute-start(bf16[128,128]{1,0:T(8,128)(2,1)S(1)} %get-tuple-element.184), channel_id=1, source_target_pairs={{33,66},{34,65},{35,68},{36,67},{37,70},{38,69},{39,72},{40,71},{4... | collective-permute-start | bytes 98312 | tf_op jit(solution)/shard_map/ppermute | solution.py:192
  60.7 4.7 %collective-permute-start.44 = (bf16[128,128]{1,0:T(8,128)(2,1)S(1)}, bf16[128,128]{1,0:T(8,128)(2,1)S(1)}, u32[]{:S(2)}, u32[]{:S(2)}) collective-permute-start(bf16[128,128]{1,0:T(8,128)(2,1)S(1)} %get-tuple-element.185), channel_id=1, source_target_pairs={{32,65},{33,64},{34,67},{35,66},{36,69},{37,68},{38,71},{39,70},{4... | collective-permute-start | bytes 98312 | tf_op jit(solution)/shard_map/ppermute | solution.py:193
  61.4 28.5 %collective-permute-start.51 = (bf16[128,768]{1,0:T(8,128)(2,1)S(1)}, bf16[128,768]{1,0:T(8,128)(2,1)S(1)}, u32[]{:S(2)}, u32[]{:S(2)}) collective-permute-start(bf16[128,768]{1,0:T(8,128)(2,1)S(1)} %get-tuple-element.194), channel_id=1, source_target_pairs={{64,96},{65,97},{66,98},{67,99},{68,100},{69,101},{70,102},{71,103... | collective-permute-start | bytes 589832 | tf_op jit(solution)/shard_map/ppermute | solution.py:191
  62.7 28.8 %collective-permute-start.52 = (bf16[128,128]{1,0:T(8,128)(2,1)S(1)}, bf16[128,128]{1,0:T(8,128)(2,1)S(1)}, u32[]{:S(2)}, u32[]{:S(2)}) collective-permute-start(bf16[128,128]{1,0:T(8,128)(2,1)S(1)} %get-tuple-element.195), channel_id=1, source_target_pairs={{65,98},{66,97},{67,100},{68,99},{69,102},{70,101},{71,104},{72,10... | collective-permute-start | bytes 98312 | tf_op jit(solution)/shard_map/ppermute | solution.py:192
  64.0 27.5 %collective-permute-start.53 = (bf16[128,128]{1,0:T(8,128)(2,1)S(1)}, bf16[128,128]{1,0:T(8,128)(2,1)S(1)}, u32[]{:S(2)}, u32[]{:S(2)}) collective-permute-start(bf16[128,128]{1,0:T(8,128)(2,1)S(1)} %get-tuple-element.196), channel_id=1, source_target_pairs={{64,97},{65,96},{66,99},{67,98},{68,101},{69,100},{70,103},{71,102... | collective-permute-start | bytes 98312 | tf_op jit(solution)/shard_map/ppermute | solution.py:193
  65.4 30.4 %collective-permute-start.48 = (bf16[128,768]{1,0:T(8,128)(2,1)S(1)}, bf16[128,768]{1,0:T(8,128)(2,1)S(1)}, u32[]{:S(2)}, u32[]{:S(2)}) collective-permute-start(bf16[128,768]{1,0:T(8,128)(2,1)S(1)} %get-tuple-element.191), channel_id=1, source_target_pairs={{64,96},{65,97},{66,98},{67,99},{68,100},{69,101},{70,102},{71,103... | collective-permute-start | bytes 589832 | tf_op jit(solution)/shard_map/ppermute | solution.py:191
  66.9 30.1 %collective-permute-start.49 = (bf16[128,128]{1,0:T(8,128)(2,1)S(1)}, bf16[128,128]{1,0:T(8,128)(2,1)S(1)}, u32[]{:S(2)}, u32[]{:S(2)}) collective-permute-start(bf16[128,128]{1,0:T(8,128)(2,1)S(1)} %get-tuple-element.192), channel_id=1, source_target_pairs={{65,98},{66,97},{67,100},{68,99},{69,102},{70,101},{71,104},{72,10... | collective-permute-start | bytes 98312 | tf_op jit(solution)/shard_map/ppermute | solution.py:192
  89.9 7.1 %collective-permute-start.50 = (bf16[128,128]{1,0:T(8,128)(2,1)S(1)}, bf16[128,128]{1,0:T(8,128)(2,1)S(1)}, u32[]{:S(2)}, u32[]{:S(2)}) collective-permute-start(bf16[128,128]{1,0:T(8,128)(2,1)S(1)} %get-tuple-element.193), channel_id=1, source_target_pairs={{64,97},{65,96},{66,99},{67,98},{68,101},{69,100},{70,103},{71,102... | collective-permute-start | bytes 98312 | tf_op jit(solution)/shard_map/ppermute | solution.py:193
  91.5 6.8 %collective-permute-start.57 = (bf16[128,768]{1,0:T(8,128)(2,1)S(1)}, bf16[128,768]{1,0:T(8,128)(2,1)S(1)}, u32[]{:S(2)}, u32[]{:S(2)}) collective-permute-start(bf16[128,768]{1,0:T(8,128)(2,1)S(1)} %get-tuple-element.202), channel_id=1, source_target_pairs={{96,128},{97,129},{98,130},{99,131},{100,132},{101,133},{102,134},... | collective-permute-start | bytes 589832 | tf_op jit(solution)/shard_map/ppermute | solution.py:191
  92.2 6.8 %collective-permute-start.58 = (bf16[128,128]{1,0:T(8,128)(2,1)S(1)}, bf16[128,128]{1,0:T(8,128)(2,1)S(1)}, u32[]{:S(2)}, u32[]{:S(2)}) collective-permute-start(bf16[128,128]{1,0:T(8,128)(2,1)S(1)} %get-tuple-element.203), channel_id=1, source_target_pairs={{97,130},{98,129},{99,132},{100,131},{101,134},{102,133},{103,136}... | collective-permute-start | bytes 98312 | tf_op jit(solution)/shard_map/ppermute | solution.py:192
  97.7 3.5 %collective-permute-start.55 = (bf16[128,128]{1,0:T(8,128)(2,1)S(1)}, bf16[128,128]{1,0:T(8,128)(2,1)S(1)}, u32[]{:S(2)}, u32[]{:S(2)}) collective-permute-start(bf16[128,128]{1,0:T(8,128)(2,1)S(1)} %get-tuple-element.200), channel_id=1, source_target_pairs={{97,130},{98,129},{99,132},{100,131},{101,134},{102,133},{103,136}... | collective-permute-start | bytes 98312 | tf_op jit(solution)/shard_map/ppermute | solution.py:192
  99.7 3.5 %collective-permute-start.64 = (bf16[128,128]{1,0:T(8,128)(2,1)S(1)}, bf16[128,128]{1,0:T(8,128)(2,1)S(1)}, u32[]{:S(2)}, u32[]{:S(2)}) collective-permute-start(bf16[128,128]{1,0:T(8,128)(2,1)S(1)} %get-tuple-element.211), channel_id=1, source_target_pairs={{129,162},{130,161},{131,164},{132,163},{133,166},{134,165},{135,1... | collective-permute-start | bytes 98312 | tf_op jit(solution)/shard_map/ppermute | solution.py:192
  101.8 3.5 %collective-permute-start.61 = (bf16[128,128]{1,0:T(8,128)(2,1)S(1)}, bf16[128,128]{1,0:T(8,128)(2,1)S(1)}, u32[]{:S(2)}, u32[]{:S(2)}) collective-permute-start(bf16[128,128]{1,0:T(8,128)(2,1)S(1)} %get-tuple-element.208), channel_id=1, source_target_pairs={{129,162},{130,161},{131,164},{132,163},{133,166},{134,165},{135,1... | collective-permute-start | bytes 98312 | tf_op jit(solution)/shard_map/ppermute | solution.py:192
  113.7 4.7 %collective-permute-start.78 = (bf16[128,768]{1,0:T(8,128)(2,1)S(1)}, bf16[128,768]{1,0:T(8,128)(2,1)S(1)}, u32[]{:S(2)}, u32[]{:S(2)}) collective-permute-start(bf16[128,768]{1,0:T(8,128)(2,1)S(1)} %get-tuple-element.231), channel_id=1, source_target_pairs={{32,64},{33,65},{34,66},{35,67},{36,68},{37,69},{38,70},{39,71},{4... | collective-permute-start | bytes 589832 | tf_op jit(solution)/shard_map/ppermute | solution.py:191
  114.4 5.3 %collective-permute-start.79 = (bf16[128,128]{1,0:T(8,128)(2,1)S(1)}, bf16[128,128]{1,0:T(8,128)(2,1)S(1)}, u32[]{:S(2)}, u32[]{:S(2)}) collective-permute-start(bf16[128,128]{1,0:T(8,128)(2,1)S(1)} %get-tuple-element.232), channel_id=1, source_target_pairs={{33,66},{34,65},{35,68},{36,67},{37,70},{38,69},{39,72},{40,71},{4... | collective-permute-start | bytes 98312 | tf_op jit(solution)/shard_map/ppermute | solution.py:192
  115.1 4.7 %collective-permute-start.80 = (bf16[128,128]{1,0:T(8,128)(2,1)S(1)}, bf16[128,128]{1,0:T(8,128)(2,1)S(1)}, u32[]{:S(2)}, u32[]{:S(2)}) collective-permute-start(bf16[128,128]{1,0:T(8,128)(2,1)S(1)} %get-tuple-element.233), channel_id=1, source_target_pairs={{32,65},{33,64},{34,67},{35,66},{36,69},{37,68},{38,71},{39,70},{4... | collective-permute-start | bytes 98312 | tf_op jit(solution)/shard_map/ppermute | solution.py:193
  115.8 30.8 %collective-permute-start.88 = (bf16[128,128]{1,0:T(8,128)(2,1)S(1)}, bf16[128,128]{1,0:T(8,128)(2,1)S(1)}, u32[]{:S(2)}, u32[]{:S(2)}) collective-permute-start(bf16[128,128]{1,0:T(8,128)(2,1)S(1)} %get-tuple-element.243), channel_id=1, source_target_pairs={{65,98},{66,97},{67,100},{68,99},{69,102},{70,101},{71,104},{72,10... | collective-permute-start | bytes 98312 | tf_op jit(solution)/shard_map/ppermute | solution.py:192
  117.1 28.2 %collective-permute-start.87 = (bf16[128,768]{1,0:T(8,128)(2,1)S(1)}, bf16[128,768]{1,0:T(8,128)(2,1)S(1)}, u32[]{:S(2)}, u32[]{:S(2)}) collective-permute-start(bf16[128,768]{1,0:T(8,128)(2,1)S(1)} %get-tuple-element.242), channel_id=1, source_target_pairs={{64,96},{65,97},{66,98},{67,99},{68,100},{69,101},{70,102},{71,103... | collective-permute-start | bytes 589832 | tf_op jit(solution)/shard_map/ppermute | solution.py:191
  118.4 28.2 %collective-permute-start.89 = (bf16[128,128]{1,0:T(8,128)(2,1)S(1)}, bf16[128,128]{1,0:T(8,128)(2,1)S(1)}, u32[]{:S(2)}, u32[]{:S(2)}) collective-permute-start(bf16[128,128]{1,0:T(8,128)(2,1)S(1)} %get-tuple-element.244), channel_id=1, source_target_pairs={{64,97},{65,96},{66,99},{67,98},{68,101},{69,100},{70,103},{71,102... | collective-permute-start | bytes 98312 | tf_op jit(solution)/shard_map/ppermute | solution.py:193
  119.8 29.9 %collective-permute-start.84 = (bf16[128,768]{1,0:T(8,128)(2,1)S(1)}, bf16[128,768]{1,0:T(8,128)(2,1)S(1)}, u32[]{:S(2)}, u32[]{:S(2)}) collective-permute-start(bf16[128,768]{1,0:T(8,128)(2,1)S(1)} %get-tuple-element.239), channel_id=1, source_target_pairs={{64,96},{65,97},{66,98},{67,99},{68,100},{69,101},{70,102},{71,103... | collective-permute-start | bytes 589832 | tf_op jit(solution)/shard_map/ppermute | solution.py:191
  121.1 30.5 %collective-permute-start.85 = (bf16[128,128]{1,0:T(8,128)(2,1)S(1)}, bf16[128,128]{1,0:T(8,128)(2,1)S(1)}, u32[]{:S(2)}, u32[]{:S(2)}) collective-permute-start(bf16[128,128]{1,0:T(8,128)(2,1)S(1)} %get-tuple-element.240), channel_id=1, source_target_pairs={{65,98},{66,97},{67,100},{68,99},{69,102},{70,101},{71,104},{72,10... | collective-permute-start | bytes 98312 | tf_op jit(solution)/shard_map/ppermute | solution.py:192
  145.3 6.2 %collective-permute-start.86 = (bf16[128,128]{1,0:T(8,128)(2,1)S(1)}, bf16[128,128]{1,0:T(8,128)(2,1)S(1)}, u32[]{:S(2)}, u32[]{:S(2)}) collective-permute-start(bf16[128,128]{1,0:T(8,128)(2,1)S(1)} %get-tuple-element.241), channel_id=1, source_target_pairs={{64,97},{65,96},{66,99},{67,98},{68,101},{69,100},{70,103},{71,102... | collective-permute-start | bytes 98312 | tf_op jit(solution)/shard_map/ppermute | solution.py:193
  (42 other events, 132.6 us)

commit v3 on v2

--- a/solution.py
+++ b/solution.py
@@ -168,7 +168,7 @@
             out_specs=[vmem] * len(results),
             input_output_aliases={len(operands) - 1: len(results) - 1},
             compiler_params=params,
-            cost_estimate=pl.CostEstimate(flops=1900000000, bytes_accessed=0, transcendentals=0),
+            cost_estimate=pl.CostEstimate(flops=1900000000 if tick else 1, bytes_accessed=0, transcendentals=0),
             name="step",
         )(*operands)
 

time: 154 us -> 154 us (level)
    ppermute x30, waiting for transfers between devices: 65.7 us -> 64 us  [local(): lax.ppermute(own, ('sec', 'row'), route(tick, lambda d: d))]
    ppermute x30, waiting for transfers between devices: 3.73 us -> 5.43 us  [local(): lax.ppermute(cross, ('sec', 'row'), route(tick, lambda d: d + 1 if d % 2...]
  transfers between devices with their start and end apart: 90 -> 90, of which waited for: 10 -> 11; matrix products, arithmetic and copies ran while one was open for 0% -> 0% of each run, Pallas kernels for 4% -> 4%
where the time goes in v3:
time: 154 us; the launch traced here: 153 us
  starting transfers between devices  71.3 us (46%)
  waiting for transfers between devices  69.5 us (45%)
  Pallas kernels  10.2 us (7%)
  between operations  1.77 us (1%)
    ppermute x30, waiting for transfers between devices, local(): lax.ppermute(own, ('sec', 'row'), route(tick, lambda d: d))  64 us
    ppermute x30, starting transfers between devices, local(): lax.ppermute(own, ('sec', 'row'), route(tick, lambda d: d))  24 us
    ppermute x30, starting transfers between devices, local(): lax.ppermute(cross, ('sec', 'row'), route(tick, lambda d: d + 1 if d % 2...  23.7 us
    ppermute x30, starting transfers between devices, local(): lax.ppermute(mate, ('sec', 'row'), route(tick, lambda d: d ^ 1))  23.6 us
    pallas_call x2, Pallas kernels, prepared(): pl.pallas_call(kernel, out_shape=pltpu.VMEM((rows, BD * BLK), bf16), in_s...  7.94 us
    ppermute x30, waiting for transfers between devices, local(): lax.ppermute(cross, ('sec', 'row'), route(tick, lambda d: d + 1 if d % 2...  5.43 us
  transfers between devices with their start and end apart: 90, of which 11 were waited for; matrix products, arithmetic and copies ran while one was open for 0% of the time, Pallas kernels for 4%

profile of v3, /device:TPU:482, one launch (start us, length us, event | category | flops | bytes accessed | tf_op | source)
XLA Modules:
  0.0 152.7 jit_solution(568314807796276904)
XLA Ops:
  0.0 2.7 %sides.1.refs_0_ = bf16[256,768]{1,0:T(8,128)(2,1)S(1)} custom-call(bf16[6,128,256]{2,1,0:T(8,128)(2,1)} %rhs_hbm.1, bf16[6,128,128]{2,1,0:T(8,128)(2,1)} %inv_hbm.3, bf16[15,128,128]{2,1,0:T(8,128)(2,1)} %sup_hbm.3), custom_call_target="tpu_custom_call" | custom-call | flops 268435456 | bytes 2097152 | tf_op jit(solution)/shard_map/sides/pallas_call | solution.py:123
  2.8 0.7 collective-permute-start.3
  4.8 5.2 %matrix.1.refs_0_.refs_3_ = bf16[1024,768]{1,0:T(8,128)(2,1)S(1)} custom-call(s32[6,5]{1,0:T(8,128)} %pattern_hbm.1, bf16[6,128,128]{2,1,0:T(8,128)(2,1)} %inv_hbm.3, bf16[6,5,128,128]{3,2,1,0:T(8,128)(2,1)} %cpl_hbm.1, bf16[15,128,128]{2,1,0:T(8,128)(2,1)} %sup_hbm.3), custom_call_target="tpu_custom_call" | custom-call | flops 1900000000 | bytes 2097152 | tf_op jit(solution)/shard_map/matrix/pallas_call | solution.py:123
  10.0 0.7 collective-permute-start
  12.1 0.7 collective-permute-start.9
  14.2 0.7 collective-permute-start.6
  16.3 1.3 collective-permute-start.15
  17.6 1.3 collective-permute-start.16
  18.9 1.3 collective-permute-start.17
  20.3 1.3 collective-permute-start.12
  21.6 1.3 collective-permute-start.13
  22.9 9.7 %collective-permute-done.15._ = bf16[128,768]{1,0:T(8,128)(2,1)S(1)} collective-permute-done((bf16[128,768]{1,0:T(8,128)(2,1)S(1)}, bf16[128,768]{1,0:T(8,128)(2,1)S(1)}, u32[]{:S(2)}, u32[]{:S(2)}) %collective-permute-start.15) | collective-permute-done | bytes 196640 | tf_op jit(solution)/shard_map/ppermute | solution.py:191
  32.5 1.3 collective-permute-start.14
  33.8 1.9 %collective-permute-done.16.refs_1_ = bf16[128,128]{1,0:T(8,128)(2,1)S(1)} collective-permute-done((bf16[128,128]{1,0:T(8,128)(2,1)S(1)}, bf16[128,128]{1,0:T(8,128)(2,1)S(1)}, u32[]{:S(2)}, u32[]{:S(2)}) %collective-permute-start.16) | collective-permute-done | bytes 32800 | tf_op jit(solution)/shard_map/ppermute | solution.py:192
  37.1 3.8 %collective-permute-done.12._ = bf16[128,768]{1,0:T(8,128)(2,1)S(1)} collective-permute-done((bf16[128,768]{1,0:T(8,128)(2,1)S(1)}, bf16[128,768]{1,0:T(8,128)(2,1)S(1)}, u32[]{:S(2)}, u32[]{:S(2)}) %collective-permute-start.12) | collective-permute-done | bytes 196640 | tf_op jit(solution)/shard_map/ppermute | solution.py:191
  41.5 1.0 collective-permute-done.13.refs_1_
  44.7 0.7 collective-permute-start.27
  46.8 0.7 collective-permute-start.24
  48.9 0.7 collective-permute-start.33
  51.0 0.7 collective-permute-start.30
  53.0 0.7 collective-permute-start.39
  55.1 0.7 collective-permute-start.36
  57.2 0.7 collective-permute-start.45
  61.4 1.3 collective-permute-start.51
  62.7 1.3 collective-permute-start.52
  64.0 1.3 collective-permute-start.53
  65.4 1.5 collective-permute-start.48
  66.9 1.3 collective-permute-start.49
  68.2 21.7 %collective-permute-done.51._ = bf16[128,768]{1,0:T(8,128)(2,1)S(1)} collective-permute-done((bf16[128,768]{1,0:T(8,128)(2,1)S(1)}, bf16[128,768]{1,0:T(8,128)(2,1)S(1)}, u32[]{:S(2)}, u32[]{:S(2)}) %collective-permute-start.51) | collective-permute-done | bytes 196640 | tf_op jit(solution)/shard_map/ppermute | solution.py:191
  89.9 1.3 collective-permute-start.50
  92.7 3.2 %collective-permute-done.48._ = bf16[128,768]{1,0:T(8,128)(2,1)S(1)} collective-permute-done((bf16[128,768]{1,0:T(8,128)(2,1)S(1)}, bf16[128,768]{1,0:T(8,128)(2,1)S(1)}, u32[]{:S(2)}, u32[]{:S(2)}) %collective-permute-start.48) | collective-permute-done | bytes 196640 | tf_op jit(solution)/shard_map/ppermute | solution.py:191
  99.1 0.7 collective-permute-start.63
  101.2 0.7 collective-permute-start.60
  103.2 0.7 collective-permute-start.69
  105.3 0.7 collective-permute-start.66
  107.4 0.7 collective-permute-start.75
  109.5 0.7 collective-permute-start.72
  111.6 0.7 collective-permute-start.81
  115.8 1.3 collective-permute-start.88
  117.1 1.3 collective-permute-start.87
  118.4 1.3 collective-permute-start.89
  119.8 1.3 collective-permute-start.84
  121.1 1.3 collective-permute-start.85
  122.4 22.9 %collective-permute-done.87._ = bf16[128,768]{1,0:T(8,128)(2,1)S(1)} collective-permute-done((bf16[128,768]{1,0:T(8,128)(2,1)S(1)}, bf16[128,768]{1,0:T(8,128)(2,1)S(1)}, u32[]{:S(2)}, u32[]{:S(2)}) %collective-permute-start.87) | collective-permute-done | bytes 196640 | tf_op jit(solution)/shard_map/ppermute | solution.py:191
  145.2 1.3 collective-permute-start.86
  146.9 2.7 %collective-permute-done.84._ = bf16[128,768]{1,0:T(8,128)(2,1)S(1)} collective-permute-done((bf16[128,768]{1,0:T(8,128)(2,1)S(1)}, bf16[128,768]{1,0:T(8,128)(2,1)S(1)}, u32[]{:S(2)}, u32[]{:S(2)}) %collective-permute-start.84) | collective-permute-done | bytes 196640 | tf_op jit(solution)/shard_map/ppermute | solution.py:191
  149.6 1.8 %collective-permute-done.85.refs_1_ = bf16[128,128]{1,0:T(8,128)(2,1)S(1)} collective-permute-done((bf16[128,128]{1,0:T(8,128)(2,1)S(1)}, bf16[128,128]{1,0:T(8,128)(2,1)S(1)}, u32[]{:S(2)}, u32[]{:S(2)}) %collective-permute-start.85) | collective-permute-done | bytes 32800 | tf_op jit(solution)/shard_map/ppermute | solution.py:192
  151.5 1.3 step.63
  (196 shorter events, 37.5 us)
Async XLA Ops:
  2.8 8.6 %collective-permute-start.3 = (bf16[128,768]{1,0:T(8,128)(2,1)S(1)}, bf16[128,768]{1,0:T(8,128)(2,1)S(1)}, u32[]{:S(2)}, u32[]{:S(2)}) collective-permute-start(bf16[128,768]{1,0:T(8,128)(2,1)S(1)} %get-tuple-element.130), channel_id=1, source_target_pairs={{0,32},{1,33},{2,34},{3,35},{4,36},{5,37},{6,38},{7,39},{8,40},{9,... | collective-permute-start | bytes 589832 | tf_op jit(solution)/shard_map/ppermute | solution.py:191
  3.4 8.6 %collective-permute-start.4 = (bf16[128,128]{1,0:T(8,128)(2,1)S(1)}, bf16[128,128]{1,0:T(8,128)(2,1)S(1)}, u32[]{:S(2)}, u32[]{:S(2)}) collective-permute-start(bf16[128,128]{1,0:T(8,128)(2,1)S(1)} %get-tuple-element.131), channel_id=1, source_target_pairs={{1,34},{2,33},{3,36},{4,35},{5,38},{6,37},{7,40},{8,39},{9,42},{10... | collective-permute-start | bytes 98312 | tf_op jit(solution)/shard_map/ppermute | solution.py:192
  4.1 8.0 %collective-permute-start.5 = (bf16[128,128]{1,0:T(8,128)(2,1)S(1)}, bf16[128,128]{1,0:T(8,128)(2,1)S(1)}, u32[]{:S(2)}, u32[]{:S(2)}) collective-permute-start(bf16[128,128]{1,0:T(8,128)(2,1)S(1)} %get-tuple-element.132), channel_id=1, source_target_pairs={{0,33},{1,32},{2,35},{3,34},{4,37},{5,36},{6,39},{7,38},{8,41},{9,... | collective-permute-start | bytes 98312 | tf_op jit(solution)/shard_map/ppermute | solution.py:193
  10.7 3.5 %collective-permute-start.1 = (bf16[128,128]{1,0:T(8,128)(2,1)S(1)}, bf16[128,128]{1,0:T(8,128)(2,1)S(1)}, u32[]{:S(2)}, u32[]{:S(2)}) collective-permute-start(bf16[128,128]{1,0:T(8,128)(2,1)S(1)} %get-tuple-element.128), channel_id=1, source_target_pairs={{1,34},{2,33},{3,36},{4,35},{5,38},{6,37},{7,40},{8,39},{9,42},{10... | collective-permute-start | bytes 98312 | tf_op jit(solution)/shard_map/ppermute | solution.py:192
  12.8 3.5 %collective-permute-start.10 = (bf16[128,128]{1,0:T(8,128)(2,1)S(1)}, bf16[128,128]{1,0:T(8,128)(2,1)S(1)}, u32[]{:S(2)}, u32[]{:S(2)}) collective-permute-start(bf16[128,128]{1,0:T(8,128)(2,1)S(1)} %get-tuple-element.139), channel_id=1, source_target_pairs={{33,66},{34,65},{35,68},{36,67},{37,70},{38,69},{39,72},{40,71},{4... | collective-permute-start | bytes 98312 | tf_op jit(solution)/shard_map/ppermute | solution.py:192
  14.2 4.7 %collective-permute-start.6 = (bf16[128,768]{1,0:T(8,128)(2,1)S(1)}, bf16[128,768]{1,0:T(8,128)(2,1)S(1)}, u32[]{:S(2)}, u32[]{:S(2)}) collective-permute-start(bf16[128,768]{1,0:T(8,128)(2,1)S(1)} %get-tuple-element.135), channel_id=1, source_target_pairs={{32,64},{33,65},{34,66},{35,67},{36,68},{37,69},{38,70},{39,71},{4... | collective-permute-start | bytes 589832 | tf_op jit(solution)/shard_map/ppermute | solution.py:191
  14.9 5.3 %collective-permute-start.7 = (bf16[128,128]{1,0:T(8,128)(2,1)S(1)}, bf16[128,128]{1,0:T(8,128)(2,1)S(1)}, u32[]{:S(2)}, u32[]{:S(2)}) collective-permute-start(bf16[128,128]{1,0:T(8,128)(2,1)S(1)} %get-tuple-element.136), channel_id=1, source_target_pairs={{33,66},{34,65},{35,68},{36,67},{37,70},{38,69},{39,72},{40,71},{4... | collective-permute-start | bytes 98312 | tf_op jit(solution)/shard_map/ppermute | solution.py:192
  15.6 4.7 %collective-permute-start.8 = (bf16[128,128]{1,0:T(8,128)(2,1)S(1)}, bf16[128,128]{1,0:T(8,128)(2,1)S(1)}, u32[]{:S(2)}, u32[]{:S(2)}) collective-permute-start(bf16[128,128]{1,0:T(8,128)(2,1)S(1)} %get-tuple-element.137), channel_id=1, source_target_pairs={{32,65},{33,64},{34,67},{35,66},{36,69},{37,68},{38,71},{39,70},{4... | collective-permute-start | bytes 98312 | tf_op jit(solution)/shard_map/ppermute | solution.py:193
  16.3 16.2 %collective-permute-start.15 = (bf16[128,768]{1,0:T(8,128)(2,1)S(1)}, bf16[128,768]{1,0:T(8,128)(2,1)S(1)}, u32[]{:S(2)}, u32[]{:S(2)}) collective-permute-start(bf16[128,768]{1,0:T(8,128)(2,1)S(1)} %get-tuple-element.146), channel_id=1, source_target_pairs={{64,96},{65,97},{66,98},{67,99},{68,100},{69,101},{70,102},{71,103... | collective-permute-start | bytes 589832 | tf_op jit(solution)/shard_map/ppermute | solution.py:191
  17.6 18.1 %collective-permute-start.16 = (bf16[128,128]{1,0:T(8,128)(2,1)S(1)}, bf16[128,128]{1,0:T(8,128)(2,1)S(1)}, u32[]{:S(2)}, u32[]{:S(2)}) collective-permute-start(bf16[128,128]{1,0:T(8,128)(2,1)S(1)} %get-tuple-element.147), channel_id=1, source_target_pairs={{65,98},{66,97},{67,100},{68,99},{69,102},{70,101},{71,104},{72,10... | collective-permute-start | bytes 98312 | tf_op jit(solution)/shard_map/ppermute | solution.py:192
  18.9 16.8 %collective-permute-start.17 = (bf16[128,128]{1,0:T(8,128)(2,1)S(1)}, bf16[128,128]{1,0:T(8,128)(2,1)S(1)}, u32[]{:S(2)}, u32[]{:S(2)}) collective-permute-start(bf16[128,128]{1,0:T(8,128)(2,1)S(1)} %get-tuple-element.148), channel_id=1, source_target_pairs={{64,97},{65,96},{66,99},{67,98},{68,101},{69,100},{70,103},{71,102... | collective-permute-start | bytes 98312 | tf_op jit(solution)/shard_map/ppermute | solution.py:193
  20.3 20.6 %collective-permute-start.12 = (bf16[128,768]{1,0:T(8,128)(2,1)S(1)}, bf16[128,768]{1,0:T(8,128)(2,1)S(1)}, u32[]{:S(2)}, u32[]{:S(2)}) collective-permute-start(bf16[128,768]{1,0:T(8,128)(2,1)S(1)} %get-tuple-element.143), channel_id=1, source_target_pairs={{64,96},{65,97},{66,98},{67,99},{68,100},{69,101},{70,102},{71,103... | collective-permute-start | bytes 589832 | tf_op jit(solution)/shard_map/ppermute | solution.py:191
  21.6 21.0 %collective-permute-start.13 = (bf16[128,128]{1,0:T(8,128)(2,1)S(1)}, bf16[128,128]{1,0:T(8,128)(2,1)S(1)}, u32[]{:S(2)}, u32[]{:S(2)}) collective-permute-start(bf16[128,128]{1,0:T(8,128)(2,1)S(1)} %get-tuple-element.144), channel_id=1, source_target_pairs={{65,98},{66,97},{67,100},{68,99},{69,102},{70,101},{71,104},{72,10... | collective-permute-start | bytes 98312 | tf_op jit(solution)/shard_map/ppermute | solution.py:192
  32.5 10.1 %collective-permute-start.14 = (bf16[128,128]{1,0:T(8,128)(2,1)S(1)}, bf16[128,128]{1,0:T(8,128)(2,1)S(1)}, u32[]{:S(2)}, u32[]{:S(2)}) collective-permute-start(bf16[128,128]{1,0:T(8,128)(2,1)S(1)} %get-tuple-element.145), channel_id=1, source_target_pairs={{64,97},{65,96},{66,99},{67,98},{68,101},{69,100},{70,103},{71,102... | collective-permute-start | bytes 98312 | tf_op jit(solution)/shard_map/ppermute | solution.py:193
  35.7 8.2 %collective-permute-start.21 = (bf16[128,768]{1,0:T(8,128)(2,1)S(1)}, bf16[128,768]{1,0:T(8,128)(2,1)S(1)}, u32[]{:S(2)}, u32[]{:S(2)}) collective-permute-start(bf16[128,768]{1,0:T(8,128)(2,1)S(1)} %get-tuple-element.154), channel_id=1, source_target_pairs={{96,128},{97,129},{98,130},{99,131},{100,132},{101,133},{102,134},... | collective-permute-start | bytes 589832 | tf_op jit(solution)/shard_map/ppermute | solution.py:191
  36.4 8.2 %collective-permute-start.22 = (bf16[128,128]{1,0:T(8,128)(2,1)S(1)}, bf16[128,128]{1,0:T(8,128)(2,1)S(1)}, u32[]{:S(2)}, u32[]{:S(2)}) collective-permute-start(bf16[128,128]{1,0:T(8,128)(2,1)S(1)} %get-tuple-element.155), channel_id=1, source_target_pairs={{97,130},{98,129},{99,132},{100,131},{101,134},{102,133},{103,136}... | collective-permute-start | bytes 98312 | tf_op jit(solution)/shard_map/ppermute | solution.py:192
  40.9 3.8 %collective-permute-start.23 = (bf16[128,128]{1,0:T(8,128)(2,1)S(1)}, bf16[128,128]{1,0:T(8,128)(2,1)S(1)}, u32[]{:S(2)}, u32[]{:S(2)}) collective-permute-start(bf16[128,128]{1,0:T(8,128)(2,1)S(1)} %get-tuple-element.156), channel_id=1, source_target_pairs={{96,129},{97,128},{98,131},{99,130},{100,133},{101,132},{102,135},... | collective-permute-start | bytes 98312 | tf_op jit(solution)/shard_map/ppermute | solution.py:193
  43.3 3.5 %collective-permute-start.19 = (bf16[128,128]{1,0:T(8,128)(2,1)S(1)}, bf16[128,128]{1,0:T(8,128)(2,1)S(1)}, u32[]{:S(2)}, u32[]{:S(2)}) collective-permute-start(bf16[128,128]{1,0:T(8,128)(2,1)S(1)} %get-tuple-element.152), channel_id=1, source_target_pairs={{97,130},{98,129},{99,132},{100,131},{101,134},{102,133},{103,136}... | collective-permute-start | bytes 98312 | tf_op jit(solution)/shard_map/ppermute | solution.py:192
  45.4 3.5 %collective-permute-start.28 = (bf16[128,128]{1,0:T(8,128)(2,1)S(1)}, bf16[128,128]{1,0:T(8,128)(2,1)S(1)}, u32[]{:S(2)}, u32[]{:S(2)}) collective-permute-start(bf16[128,128]{1,0:T(8,128)(2,1)S(1)} %get-tuple-element.163), channel_id=1, source_target_pairs={{129,162},{130,161},{131,164},{132,163},{133,166},{134,165},{135,1... | collective-permute-start | bytes 98312 | tf_op jit(solution)/shard_map/ppermute | solution.py:192
  47.5 3.5 %collective-permute-start.25 = (bf16[128,128]{1,0:T(8,128)(2,1)S(1)}, bf16[128,128]{1,0:T(8,128)(2,1)S(1)}, u32[]{:S(2)}, u32[]{:S(2)}) collective-permute-start(bf16[128,128]{1,0:T(8,128)(2,1)S(1)} %get-tuple-element.160), channel_id=1, source_target_pairs={{129,162},{130,161},{131,164},{132,163},{133,166},{134,165},{135,1... | collective-permute-start | bytes 98312 | tf_op jit(solution)/shard_map/ppermute | solution.py:192
  49.5 3.5 %collective-permute-start.34 = (bf16[128,128]{1,0:T(8,128)(2,1)S(1)}, bf16[128,128]{1,0:T(8,128)(2,1)S(1)}, u32[]{:S(2)}, u32[]{:S(2)}) collective-permute-start(bf16[128,128]{1,0:T(8,128)(2,1)S(1)} %get-tuple-element.171), channel_id=1, source_target_pairs={{161,194},{162,193},{163,196},{164,195},{165,198},{166,197},{167,2... | collective-permute-start | bytes 98312 | tf_op jit(solution)/shard_map/ppermute | solution.py:192
  51.6 3.5 %collective-permute-start.31 = (bf16[128,128]{1,0:T(8,128)(2,1)S(1)}, bf16[128,128]{1,0:T(8,128)(2,1)S(1)}, u32[]{:S(2)}, u32[]{:S(2)}) collective-permute-start(bf16[128,128]{1,0:T(8,128)(2,1)S(1)} %get-tuple-element.168), channel_id=1, source_target_pairs={{161,194},{162,193},{163,196},{164,195},{165,198},{166,197},{167,2... | collective-permute-start | bytes 98312 | tf_op jit(solution)/shard_map/ppermute | solution.py:192
  53.7 3.5 %collective-permute-start.40 = (bf16[128,128]{1,0:T(8,128)(2,1)S(1)}, bf16[128,128]{1,0:T(8,128)(2,1)S(1)}, u32[]{:S(2)}, u32[]{:S(2)}) collective-permute-start(bf16[128,128]{1,0:T(8,128)(2,1)S(1)} %get-tuple-element.179), channel_id=1, source_target_pairs={{1,34},{2,33},{3,36},{4,35},{5,38},{6,37},{7,40},{8,39},{9,42},{10... | collective-permute-start | bytes 98312 | tf_op jit(solution)/shard_map/ppermute | solution.py:192
  55.8 3.5 %collective-permute-start.37 = (bf16[128,128]{1,0:T(8,128)(2,1)S(1)}, bf16[128,128]{1,0:T(8,128)(2,1)S(1)}, u32[]{:S(2)}, u32[]{:S(2)}) collective-permute-start(bf16[128,128]{1,0:T(8,128)(2,1)S(1)} %get-tuple-element.176), channel_id=1, source_target_pairs={{1,34},{2,33},{3,36},{4,35},{5,38},{6,37},{7,40},{8,39},{9,42},{10... | collective-permute-start | bytes 98312 | tf_op jit(solution)/shard_map/ppermute | solution.py:192
  57.9 3.5 %collective-permute-start.46 = (bf16[128,128]{1,0:T(8,128)(2,1)S(1)}, bf16[128,128]{1,0:T(8,128)(2,1)S(1)}, u32[]{:S(2)}, u32[]{:S(2)}) collective-permute-start(bf16[128,128]{1,0:T(8,128)(2,1)S(1)} %get-tuple-element.187), channel_id=1, source_target_pairs={{33,66},{34,65},{35,68},{36,67},{37,70},{38,69},{39,72},{40,71},{4... | collective-permute-start | bytes 98312 | tf_op jit(solution)/shard_map/ppermute | solution.py:192
  59.3 4.7 %collective-permute-start.42 = (bf16[128,768]{1,0:T(8,128)(2,1)S(1)}, bf16[128,768]{1,0:T(8,128)(2,1)S(1)}, u32[]{:S(2)}, u32[]{:S(2)}) collective-permute-start(bf16[128,768]{1,0:T(8,128)(2,1)S(1)} %get-tuple-element.183), channel_id=1, source_target_pairs={{32,64},{33,65},{34,66},{35,67},{36,68},{37,69},{38,70},{39,71},{4... | collective-permute-start | bytes 589832 | tf_op jit(solution)/shard_map/ppermute | solution.py:191
  60.0 5.3 %collective-permute-start.43 = (bf16[128,128]{1,0:T(8,128)(2,1)S(1)}, bf16[128,128]{1,0:T(8,128)(2,1)S(1)}, u32[]{:S(2)}, u32[]{:S(2)}) collective-permute-start(bf16[128,128]{1,0:T(8,128)(2,1)S(1)} %get-tuple-element.184), channel_id=1, source_target_pairs={{33,66},{34,65},{35,68},{36,67},{37,70},{38,69},{39,72},{40,71},{4... | collective-permute-start | bytes 98312 | tf_op jit(solution)/shard_map/ppermute | solution.py:192
  60.7 4.7 %collective-permute-start.44 = (bf16[128,128]{1,0:T(8,128)(2,1)S(1)}, bf16[128,128]{1,0:T(8,128)(2,1)S(1)}, u32[]{:S(2)}, u32[]{:S(2)}) collective-permute-start(bf16[128,128]{1,0:T(8,128)(2,1)S(1)} %get-tuple-element.185), channel_id=1, source_target_pairs={{32,65},{33,64},{34,67},{35,66},{36,69},{37,68},{38,71},{39,70},{4... | collective-permute-start | bytes 98312 | tf_op jit(solution)/shard_map/ppermute | solution.py:193
  61.4 28.5 %collective-permute-start.51 = (bf16[128,768]{1,0:T(8,128)(2,1)S(1)}, bf16[128,768]{1,0:T(8,128)(2,1)S(1)}, u32[]{:S(2)}, u32[]{:S(2)}) collective-permute-start(bf16[128,768]{1,0:T(8,128)(2,1)S(1)} %get-tuple-element.194), channel_id=1, source_target_pairs={{64,96},{65,97},{66,98},{67,99},{68,100},{69,101},{70,102},{71,103... | collective-permute-start | bytes 589832 | tf_op jit(solution)/shard_map/ppermute | solution.py:191
  62.7 28.6 %collective-permute-start.52 = (bf16[128,128]{1,0:T(8,128)(2,1)S(1)}, bf16[128,128]{1,0:T(8,128)(2,1)S(1)}, u32[]{:S(2)}, u32[]{:S(2)}) collective-permute-start(bf16[128,128]{1,0:T(8,128)(2,1)S(1)} %get-tuple-element.195), channel_id=1, source_target_pairs={{65,98},{66,97},{67,100},{68,99},{69,102},{70,101},{71,104},{72,10... | collective-permute-start | bytes 98312 | tf_op jit(solution)/shard_map/ppermute | solution.py:192
  64.0 27.3 %collective-permute-start.53 = (bf16[128,128]{1,0:T(8,128)(2,1)S(1)}, bf16[128,128]{1,0:T(8,128)(2,1)S(1)}, u32[]{:S(2)}, u32[]{:S(2)}) collective-permute-start(bf16[128,128]{1,0:T(8,128)(2,1)S(1)} %get-tuple-element.196), channel_id=1, source_target_pairs={{64,97},{65,96},{66,99},{67,98},{68,101},{69,100},{70,103},{71,102... | collective-permute-start | bytes 98312 | tf_op jit(solution)/shard_map/ppermute | solution.py:193
  65.4 30.5 %collective-permute-start.48 = (bf16[128,768]{1,0:T(8,128)(2,1)S(1)}, bf16[128,768]{1,0:T(8,128)(2,1)S(1)}, u32[]{:S(2)}, u32[]{:S(2)}) collective-permute-start(bf16[128,768]{1,0:T(8,128)(2,1)S(1)} %get-tuple-element.191), channel_id=1, source_target_pairs={{64,96},{65,97},{66,98},{67,99},{68,100},{69,101},{70,102},{71,103... | collective-permute-start | bytes 589832 | tf_op jit(solution)/shard_map/ppermute | solution.py:191
  66.9 30.1 %collective-permute-start.49 = (bf16[128,128]{1,0:T(8,128)(2,1)S(1)}, bf16[128,128]{1,0:T(8,128)(2,1)S(1)}, u32[]{:S(2)}, u32[]{:S(2)}) collective-permute-start(bf16[128,128]{1,0:T(8,128)(2,1)S(1)} %get-tuple-element.192), channel_id=1, source_target_pairs={{65,98},{66,97},{67,100},{68,99},{69,102},{70,101},{71,104},{72,10... | collective-permute-start | bytes 98312 | tf_op jit(solution)/shard_map/ppermute | solution.py:192
  89.9 7.1 %collective-permute-start.50 = (bf16[128,128]{1,0:T(8,128)(2,1)S(1)}, bf16[128,128]{1,0:T(8,128)(2,1)S(1)}, u32[]{:S(2)}, u32[]{:S(2)}) collective-permute-start(bf16[128,128]{1,0:T(8,128)(2,1)S(1)} %get-tuple-element.193), channel_id=1, source_target_pairs={{64,97},{65,96},{66,99},{67,98},{68,101},{69,100},{70,103},{71,102... | collective-permute-start | bytes 98312 | tf_op jit(solution)/shard_map/ppermute | solution.py:193
  91.3 7.0 %collective-permute-start.57 = (bf16[128,768]{1,0:T(8,128)(2,1)S(1)}, bf16[128,768]{1,0:T(8,128)(2,1)S(1)}, u32[]{:S(2)}, u32[]{:S(2)}) collective-permute-start(bf16[128,768]{1,0:T(8,128)(2,1)S(1)} %get-tuple-element.202), channel_id=1, source_target_pairs={{96,128},{97,129},{98,130},{99,131},{100,132},{101,133},{102,134},... | collective-permute-start | bytes 589832 | tf_op jit(solution)/shard_map/ppermute | solution.py:191
  92.0 7.0 %collective-permute-start.58 = (bf16[128,128]{1,0:T(8,128)(2,1)S(1)}, bf16[128,128]{1,0:T(8,128)(2,1)S(1)}, u32[]{:S(2)}, u32[]{:S(2)}) collective-permute-start(bf16[128,128]{1,0:T(8,128)(2,1)S(1)} %get-tuple-element.203), channel_id=1, source_target_pairs={{97,130},{98,129},{99,132},{100,131},{101,134},{102,133},{103,136}... | collective-permute-start | bytes 98312 | tf_op jit(solution)/shard_map/ppermute | solution.py:192
  97.6 3.5 %collective-permute-start.55 = (bf16[128,128]{1,0:T(8,128)(2,1)S(1)}, bf16[128,128]{1,0:T(8,128)(2,1)S(1)}, u32[]{:S(2)}, u32[]{:S(2)}) collective-permute-start(bf16[128,128]{1,0:T(8,128)(2,1)S(1)} %get-tuple-element.200), channel_id=1, source_target_pairs={{97,130},{98,129},{99,132},{100,131},{101,134},{102,133},{103,136}... | collective-permute-start | bytes 98312 | tf_op jit(solution)/shard_map/ppermute | solution.py:192
  103.9 3.5 %collective-permute-start.70 = (bf16[128,128]{1,0:T(8,128)(2,1)S(1)}, bf16[128,128]{1,0:T(8,128)(2,1)S(1)}, u32[]{:S(2)}, u32[]{:S(2)}) collective-permute-start(bf16[128,128]{1,0:T(8,128)(2,1)S(1)} %get-tuple-element.219), channel_id=1, source_target_pairs={{161,194},{162,193},{163,196},{164,195},{165,198},{166,197},{167,2... | collective-permute-start | bytes 98312 | tf_op jit(solution)/shard_map/ppermute | solution.py:192
  106.0 3.5 %collective-permute-start.67 = (bf16[128,128]{1,0:T(8,128)(2,1)S(1)}, bf16[128,128]{1,0:T(8,128)(2,1)S(1)}, u32[]{:S(2)}, u32[]{:S(2)}) collective-permute-start(bf16[128,128]{1,0:T(8,128)(2,1)S(1)} %get-tuple-element.216), channel_id=1, source_target_pairs={{161,194},{162,193},{163,196},{164,195},{165,198},{166,197},{167,2... | collective-permute-start | bytes 98312 | tf_op jit(solution)/shard_map/ppermute | solution.py:192
  113.7 4.7 %collective-permute-start.78 = (bf16[128,768]{1,0:T(8,128)(2,1)S(1)}, bf16[128,768]{1,0:T(8,128)(2,1)S(1)}, u32[]{:S(2)}, u32[]{:S(2)}) collective-permute-start(bf16[128,768]{1,0:T(8,128)(2,1)S(1)} %get-tuple-element.231), channel_id=1, source_target_pairs={{32,64},{33,65},{34,66},{35,67},{36,68},{37,69},{38,70},{39,71},{4... | collective-permute-start | bytes 589832 | tf_op jit(solution)/shard_map/ppermute | solution.py:191
  114.4 5.3 %collective-permute-start.79 = (bf16[128,128]{1,0:T(8,128)(2,1)S(1)}, bf16[128,128]{1,0:T(8,128)(2,1)S(1)}, u32[]{:S(2)}, u32[]{:S(2)}) collective-permute-start(bf16[128,128]{1,0:T(8,128)(2,1)S(1)} %get-tuple-element.232), channel_id=1, source_target_pairs={{33,66},{34,65},{35,68},{36,67},{37,70},{38,69},{39,72},{40,71},{4... | collective-permute-start | bytes 98312 | tf_op jit(solution)/shard_map/ppermute | solution.py:192
  115.1 4.7 %collective-permute-start.80 = (bf16[128,128]{1,0:T(8,128)(2,1)S(1)}, bf16[128,128]{1,0:T(8,128)(2,1)S(1)}, u32[]{:S(2)}, u32[]{:S(2)}) collective-permute-start(bf16[128,128]{1,0:T(8,128)(2,1)S(1)} %get-tuple-element.233), channel_id=1, source_target_pairs={{32,65},{33,64},{34,67},{35,66},{36,69},{37,68},{38,71},{39,70},{4... | collective-permute-start | bytes 98312 | tf_op jit(solution)/shard_map/ppermute | solution.py:193
  115.8 30.7 %collective-permute-start.88 = (bf16[128,128]{1,0:T(8,128)(2,1)S(1)}, bf16[128,128]{1,0:T(8,128)(2,1)S(1)}, u32[]{:S(2)}, u32[]{:S(2)}) collective-permute-start(bf16[128,128]{1,0:T(8,128)(2,1)S(1)} %get-tuple-element.243), channel_id=1, source_target_pairs={{65,98},{66,97},{67,100},{68,99},{69,102},{70,101},{71,104},{72,10... | collective-permute-start | bytes 98312 | tf_op jit(solution)/shard_map/ppermute | solution.py:192
  117.1 28.1 %collective-permute-start.87 = (bf16[128,768]{1,0:T(8,128)(2,1)S(1)}, bf16[128,768]{1,0:T(8,128)(2,1)S(1)}, u32[]{:S(2)}, u32[]{:S(2)}) collective-permute-start(bf16[128,768]{1,0:T(8,128)(2,1)S(1)} %get-tuple-element.242), channel_id=1, source_target_pairs={{64,96},{65,97},{66,98},{67,99},{68,100},{69,101},{70,102},{71,103... | collective-permute-start | bytes 589832 | tf_op jit(solution)/shard_map/ppermute | solution.py:191
  118.4 28.1 %collective-permute-start.89 = (bf16[128,128]{1,0:T(8,128)(2,1)S(1)}, bf16[128,128]{1,0:T(8,128)(2,1)S(1)}, u32[]{:S(2)}, u32[]{:S(2)}) collective-permute-start(bf16[128,128]{1,0:T(8,128)(2,1)S(1)} %get-tuple-element.244), channel_id=1, source_target_pairs={{64,97},{65,96},{66,99},{67,98},{68,101},{69,100},{70,103},{71,102... | collective-permute-start | bytes 98312 | tf_op jit(solution)/shard_map/ppermute | solution.py:193
  119.8 29.9 %collective-permute-start.84 = (bf16[128,768]{1,0:T(8,128)(2,1)S(1)}, bf16[128,768]{1,0:T(8,128)(2,1)S(1)}, u32[]{:S(2)}, u32[]{:S(2)}) collective-permute-start(bf16[128,768]{1,0:T(8,128)(2,1)S(1)} %get-tuple-element.239), channel_id=1, source_target_pairs={{64,96},{65,97},{66,98},{67,99},{68,100},{69,101},{70,102},{71,103... | collective-permute-start | bytes 589832 | tf_op jit(solution)/shard_map/ppermute | solution.py:191
  121.1 30.4 %collective-permute-start.85 = (bf16[128,128]{1,0:T(8,128)(2,1)S(1)}, bf16[128,128]{1,0:T(8,128)(2,1)S(1)}, u32[]{:S(2)}, u32[]{:S(2)}) collective-permute-start(bf16[128,128]{1,0:T(8,128)(2,1)S(1)} %get-tuple-element.240), channel_id=1, source_target_pairs={{65,98},{66,97},{67,100},{68,99},{69,102},{70,101},{71,104},{72,10... | collective-permute-start | bytes 98312 | tf_op jit(solution)/shard_map/ppermute | solution.py:192
  145.2 6.2 %collective-permute-start.86 = (bf16[128,128]{1,0:T(8,128)(2,1)S(1)}, bf16[128,128]{1,0:T(8,128)(2,1)S(1)}, u32[]{:S(2)}, u32[]{:S(2)}) collective-permute-start(bf16[128,128]{1,0:T(8,128)(2,1)S(1)} %get-tuple-element.241), channel_id=1, source_target_pairs={{64,97},{65,96},{66,99},{67,98},{68,101},{69,100},{70,103},{71,102... | collective-permute-start | bytes 98312 | tf_op jit(solution)/shard_map/ppermute | solution.py:193
  (42 other events, 132.6 us)
